TPU v7x, 256 devices: a whole 4x4x8 slice. The times are simulated.
256 devices in a mesh: lon: 16 (over x_hi, z), lat: 8 (over y, x_lo), ch: 2 (over core).
Axes of the slice: x: 4 (x_hi: 2, x_lo: 2; x = x_hi * 2 + x_lo), y: 4, z: 8, core: 2. Of those that a mesh axis runs over, the one named last changes fastest.
Arguments:
- fields: bfloat16 [69, 512, 2048], P(None, 'lat', 'lon'), may hold values from -6 to 6
- conv_weight: bfloat16 [128, 9, 69], P('ch'), may hold values from -0.25 to 0.25
- embed_weight: bfloat16 [128, 16384], replicated, may hold values from -0.125 to 0.125
- token_grads: bfloat16 [16, 8, 512, 1024], P('lon', 'lat'), may hold values from -0.0234375 to 0.0234375
Outputs:
- embedded: bfloat16 [16, 8, 512, 1024], P('lon', 'lat', None, 'ch')
- conv_gradient: float32 [128, 9, 69], P('ch')
- embed_gradient: float32 [128, 16384], P('ch', ('lon', 'lat'))
All inputs are finite; a program needn't handle non-finite values.
Results may differ from a plain program's by a relative error of at most 0.0049.
Values may be sent and summed in bfloat16 or wider, within the bound.
A program may use at most 128 MiB of HBM per device.

v0:
```python
import jax
import jax.numpy as jnp
from jax import lax
from jax.sharding import PartitionSpec as P


def with_halo(value, sides, width):
    for axis, dim in sides:
        size, length = (lax.axis_size(axis), value.shape[dim])
        up = [(i, (i + 1) % size) for i in range(size)]
        down = [(j, i) for i, j in up]
        last = lax.slice_in_dim(value, length - width, length, axis=dim)
        initial = lax.slice_in_dim(value, 0, width, axis=dim)
        before = lax.ppermute(last, axis, up)
        after = lax.ppermute(initial, axis, down)
        value = jnp.concatenate([before, value, after], axis=dim)
    return value


def from_behind(value, axis, by):
    length = lax.axis_size(axis)
    return lax.ppermute(value, axis, [(i, (i + by) % length) for i in range(length)])


def convolve(weights, extended, row_count, col_count):
    total = jnp.zeros((weights.shape[0], row_count * col_count), jnp.float32)
    for position in range(9):
        row_shift, col_shift = divmod(position, 3)
        window = extended[:, row_shift : row_shift + row_count, col_shift : col_shift + col_count]
        total = total + jnp.dot(
            weights[:, position, :],
            window.reshape(extended.shape[0], row_count * col_count),
            preferred_element_type=jnp.float32,
        )
    return total


def weight_terms(preact_grad, extended, row_count, col_count):
    terms = []
    for position in range(9):
        row_shift, col_shift = divmod(position, 3)
        window = extended[:, row_shift : row_shift + row_count, col_shift : col_shift + col_count]
        window = window.reshape(extended.shape[0], row_count * col_count)
        terms.append(
            lax.dot_general(
                preact_grad, window, (((1,), (1,)), ((), ())), preferred_element_type=jnp.float32
            )
        )
    return jnp.stack(terms, axis=1)


def patchify(hidden, channels, row_count, col_count):
    shaped = hidden.reshape(channels, row_count // 4, 4, col_count // 4, 4)
    return shaped.transpose(1, 3, 0, 2, 4).reshape(row_count // 4 * (col_count // 4), channels * 16)


def unpatchify(patch_grad, channels, row_count, col_count):
    shaped = patch_grad.reshape(row_count // 4, col_count // 4, channels, 4, 4)
    return shaped.transpose(2, 0, 3, 1, 4).reshape(channels, row_count * col_count)


def body(fields, conv_weight, embed_weight, token_grads):
    field_count, row_count, col_count = fields.shape
    local_channels = conv_weight.shape[0]
    width = embed_weight.shape[1] // 16
    lon_count = lax.axis_size("lon")
    lat_count = lax.axis_size("lat")
    group_count = lax.axis_size("ch")
    group_index = lax.axis_index("ch")
    lat_index = lax.axis_index("lat")
    extended = with_halo(fields, (("lon", 2), ("lat", 1)), 1)
    far_top, far_bottom = from_behind(
        (extended[:, 1, :], extended[:, row_count, :]), "lon", lon_count // 2
    )
    top_row = jnp.where(lat_index == 0, far_top, extended[:, 0, :])
    bottom_row = jnp.where(lat_index == lat_count - 1, far_bottom, extended[:, row_count + 1, :])
    extended = jnp.concatenate(
        [top_row[:, None, :], extended[:, 1 : row_count + 1, :], bottom_row[:, None, :]], axis=1
    )
    preact = convolve(conv_weight, extended, row_count, col_count)
    hidden, gelu_back = jax.vjp(jax.nn.gelu, preact)
    patch_rows = patchify(
        hidden.astype(jnp.bfloat16).reshape(local_channels, row_count, col_count),
        local_channels,
        row_count,
        col_count,
    )
    embed_matrix = embed_weight.reshape(embed_weight.shape[0] * 16, width)
    own_rows = lax.dynamic_slice_in_dim(
        embed_matrix, group_index * (local_channels * 16), local_channels * 16, 0
    )
    feature_count = width // group_count
    partial_terms = jnp.dot(patch_rows, own_rows, preferred_element_type=jnp.float32)
    embedded = lax.psum_scatter(partial_terms, "ch", scatter_dimension=1, tiled=True)
    embedded = embedded.astype(jnp.bfloat16).reshape(row_count // 4, col_count // 4, feature_count)
    embedded = lax.all_to_all(embedded, "lon", split_axis=0, concat_axis=1, tiled=True)
    embedded = embedded.reshape(1, 1, embedded.shape[1], feature_count)
    incoming = token_grads.reshape(1, token_grads.shape[2], width)
    incoming = lax.all_to_all(incoming, "lon", split_axis=1, concat_axis=0, tiled=True)
    token_rows = incoming.reshape(row_count // 4 * (col_count // 4), width)
    patch_grad = lax.dot_general(
        token_rows, own_rows, (((1,), (1,)), ((), ())), preferred_element_type=jnp.float32
    )
    embed_terms = lax.dot_general(
        patch_rows, token_rows, (((0,), (0,)), ((), ())), preferred_element_type=jnp.float32
    )
    embed_gradient = lax.psum_scatter(
        embed_terms.reshape(local_channels, 16 * width),
        ("lon", "lat"),
        scatter_dimension=1,
        tiled=True,
    )
    preact_grad = gelu_back(unpatchify(patch_grad, local_channels, row_count, col_count))[0].astype(
        jnp.bfloat16
    )
    conv_terms = weight_terms(preact_grad, extended, row_count, col_count)
    conv_gradient = lax.psum(conv_terms, ("lon", "lat"))
    return (embedded, conv_gradient, embed_gradient)


def solution(mesh):
    return jax.shard_map(
        body,
        mesh=mesh,
        in_specs=(P(None, "lat", "lon"), P("ch", None, None), P(), P("lon", "lat", None, None)),
        out_specs=(P("lon", "lat", None, "ch"), P("ch", None, None), P("ch", ("lon", "lat"))),
        check_vma=False,
    )
```

profile of v0, /device:TPU:0, one launch (start us, length us, event | category | flops | bytes accessed | tf_op | source)
XLA Modules:
  0.0 884.1 jit_solution(7269562553467243017)
XLA Ops:
  8.0 3.1 copy.31
  11.4 6.5 collective-permute-start.1
  17.9 3.0 copy.55
  21.4 9.0 %reduce = bf16[512,1024]{1,0:T(8,128)(2,1)} reduce(bf16[512,1,1024]{2,1,0:T(2,128)(2,1)} %bitcast.179, bf16[]{:T(256)} %broadcast.25), dimensions={1}, to_apply=%bitcast.157.reduce_sub_computation | reduce | bytes 2097154
  30.4 2.7 reshape.95
  33.1 5.9 all-to-all-start.1
  41.6 7.4 reshape.87
  50.3 4.0 collective-permute-start.4
  54.2 2.3 collective-permute-start.5
  57.9 2.8 copy.35
  60.8 2.8 copy.34
  63.6 2.8 pad_maximum_fusion.2
  71.0 3.2 maximum_maximum_fusion
  74.1 2.6 fusion.56
  78.7 2.5 convolution_bitcast_fusion.1
  83.4 2.2 convolution_bitcast_fusion.2
  89.0 5.8 reshape.96
  94.8 4.8 fusion.16
  99.6 6.2 reshape.92
  105.8 9.5 %copy.39 = f32[64,16,4,32,4]{0,4,3,2,1:T(4,128)} copy(f32[64,16,4,32,4]{3,1,4,2,0:T(8,128)} %bitcast.158) | data formatting | bytes 4194304 | tf_op jit(solution)/shard_map/transpose | solution.py:59
  115.3 3.8 copy.40
  119.1 6.9 fusion.11
  126.0 2.8 copy.36
  128.8 9.7 %copy.37 = bf16[16,32,64,4,4]{1,0,4,3,2:T(8,128)(2,1)} copy(bf16[16,32,64,4,4]{2,4,1,3,0:T(4,128)(2,1)} %bitcast.178) | data formatting | bytes 2097152 | tf_op jit(solution)/shard_map/transpose | solution.py:54
  138.4 7.0 reshape.86
  145.4 4.5 fusion.14
  150.0 2.2 fusion.27
  160.6 5.3 fusion.28
  165.9 5.0 reshape.94
  172.3 23.6 %all_to_all.8 = bf16[16,32,512]{2,1,0:T(8,128)(2,1)S(1)} all-to-all(bf16[16,32,512]{2,1,0:T(8,128)(2,1)S(1)} %bitcast.183), channel_id=1, replica_groups=mesh['lon'=16,'lat'=8,'ch'=2] {'lon'}, dimensions={0} | all-to-all | bytes 1048576 | tf_op jit(solution)/shard_map/all_to_all | solution.py:96
  196.0 179.7 %all-reduce.2.cloned.1.call-done = f32[64,9,69]{2,0,1:T(8,128)} async-done(((f32[64,9,69]{2,0,1:T(8,128)}), f32[64,9,69]{2,0,1:T(8,128)}) %all-reduce.2.cloned.1.call-update) | async-done | bytes 158992 | tf_op jit(solution)/shard_map/psum | solution.py:117
  375.7 498.2 %reduce-scatter.5.cloned.1.call-done = f32[64,128]{1,0:T(8,128)} async-done(((f32[64,16384]{1,0:T(8,128)}), f32[64,128]{1,0:T(8,128)}) %reduce-scatter.5.cloned.1.call-update) | async-done | bytes 32784 | tf_op jit(solution)/shard_map/reduce_scatter | solution.py:107
  (81 shorter events, 30.1 us)
Async XLA Ops:
  8.0 9.9 %copy-start.15 = (bf16[1,1,512,1024]{3,2,1,0:T(8,128)(2,1)S(1)}, bf16[1,1,512,1024]{3,2,1,0:T(8,128)(2,1)}, u32[]{:S(2)}) copy-start(bf16[1,1,512,1024]{3,2,1,0:T(8,128)(2,1)} %param.7) | copy-start | bytes 3145732
  11.2 37.8 %collective-permute-start = (bf16[69,64,1]{0,2,1:T(2,128)(2,1)S(1)}, bf16[69,64,1]{0,2,1:T(2,128)(2,1)S(1)}, u32[]{:S(2)}, u32[]{:S(2)}) collective-permute-start(bf16[69,64,1]{0,2,1:T(2,128)(2,1)S(1)} %get-tuple-element.15), channel_id=1, source_target_pairs={{0,16},{16,32},{32,48},{48,64},{64,80},{80,96},{96,112},{112,128},... | collective-permute-start | bytes 26504 | tf_op jit(solution)/shard_map/ppermute | solution.py:14
  11.4 37.6 %collective-permute-start.1 = (bf16[69,64,1]{0,2,1:T(2,128)(2,1)S(1)}, bf16[69,64,1]{0,2,1:T(2,128)(2,1)S(1)}, u32[]{:S(2)}, u32[]{:S(2)}) collective-permute-start(bf16[69,64,1]{0,2,1:T(2,128)(2,1)S(1)} %get-tuple-element.16), channel_id=1, source_target_pairs={{16,0},{32,16},{48,32},{64,48},{80,64},{96,80},{112,96},{128,112},... | collective-permute-start | bytes 26504 | tf_op jit(solution)/shard_map/ppermute | solution.py:15
  30.4 9.2 %copy-start.14 = (bf16[69,64,128]{2,1,0:T(8,128)(2,1)S(1)}, bf16[69,64,128]{2,1,0:T(8,128)(2,1)}, u32[]{:S(2)}) copy-start(bf16[69,64,128]{2,1,0:T(8,128)(2,1)} %param.4) | copy-start | bytes 3391492
  33.1 55.9 %all-to-all-start.1 = ((bf16[16,2,16384]{2,1,0:T(2,128)(2,1)}), bf16[16,2,16384]{2,1,0:T(2,128)(2,1)}, u32[]{:S(2)}, u32[]{:S(2)}) async-start(bf16[16,2,16384]{2,1,0:T(2,128)(2,1)} %reshape.95), calls=%async_computation.2 | async-start | bytes 2097152 | tf_op jit(solution)/shard_map/all_to_all | solution.py:99
  39.1 132.0 %reduce-scatter.3.cloned.1.call-start = ((), (), s32[]{:S(2)}) async-start(), calls=%async_computation.4 | async-start | bytes 3145728 | tf_op jit(solution)/shard_map/reduce_scatter | solution.py:94
  49.7 21.3 %collective-permute-start.3 = (bf16[69,1,130]{0,2,1:T(8,128)(2,1)}, bf16[69,1,130]{0,2,1:T(8,128)(2,1)S(1)}, u32[]{:S(2)}, u32[]{:S(2)}) collective-permute-start(bf16[69,1,130]{0,2,1:T(8,128)(2,1)} %get-tuple-element.12), channel_id=1, source_target_pairs={{0,2},{2,4},{4,6},{6,8},{8,10},{10,12},{12,14},{14,0},{1,3},{3,5},... | collective-permute-start | bytes 53828 | tf_op jit(solution)/shard_map/ppermute | solution.py:14
  50.3 19.8 %collective-permute-start.4 = (bf16[69,130]{0,1:T(8,128)(2,1)}, bf16[69,130]{0,1:T(8,128)(2,1)S(1)}, u32[]{:S(2)}, u32[]{:S(2)}) collective-permute-start(bf16[69,130]{0,1:T(8,128)(2,1)} %bitcast.14), channel_id=1, source_target_pairs={{0,128},{16,144},{32,160},{48,176},{64,192},{80,208},{96,224},{112... | collective-permute-start | bytes 53828 | tf_op jit(solution)/shard_map/ppermute | solution.py:22
  54.2 15.9 %collective-permute-start.5 = (bf16[69,1,130]{0,2,1:T(8,128)(2,1)}, bf16[69,1,130]{0,2,1:T(8,128)(2,1)}, u32[]{:S(2)}, u32[]{:S(2)}) collective-permute-start(bf16[69,1,130]{0,2,1:T(8,128)(2,1)} %get-tuple-element.11), channel_id=1, source_target_pairs={{2,0},{4,2},{6,4},{8,6},{10,8},{12,10},{14,12},{0,14},{3,1},{5,3},... | collective-permute-start | bytes 53828 | tf_op jit(solution)/shard_map/ppermute | solution.py:15
  56.6 14.4 %collective-permute-start.2 = (bf16[69,130]{0,1:T(8,128)(2,1)}, bf16[69,130]{0,1:T(8,128)(2,1)S(1)}, u32[]{:S(2)}, u32[]{:S(2)}) collective-permute-start(bf16[69,130]{0,1:T(8,128)(2,1)} %bitcast), channel_id=1, source_target_pairs={{0,128},{16,144},{32,160},{48,176},{64,192},{80,208},{96,224},{112... | collective-permute-start | bytes 53828 | tf_op jit(solution)/shard_map/ppermute | solution.py:22
  66.4 1.0 copy-start.17
  67.4 1.9 copy-start.10
  70.1 17.2 %copy-start.12 = (bf16[9,8,64,128]{3,1,2,0:T(8,128)(2,1)}, bf16[9,8,64,128]{3,1,2,0:T(8,128)(2,1)S(1)}, u32[]{:S(2)}) copy-start(bf16[9,8,64,128]{3,1,2,0:T(8,128)(2,1)S(1)} %copy.43) | copy-start | bytes 3538948
  76.7 1.4 copy-start.4
  76.7 2.0 copy-start
  76.7 6.6 copy-start.2
  76.7 8.8 %copy-start.7 = (bf16[69,64,128]{0,2,1:T(8,128)(2,1)}, bf16[69,64,128]{0,2,1:T(8,128)(2,1)S(1)}, u32[]{:S(2)}) copy-start(bf16[69,64,128]{0,2,1:T(8,128)(2,1)S(1)} %get-tuple-element.4) | copy-start | bytes 3391492
  76.7 9.7 %copy-start.5 = (bf16[69,64,128]{0,2,1:T(8,128)(2,1)}, bf16[69,64,128]{0,2,1:T(8,128)(2,1)S(1)}, u32[]{:S(2)}) copy-start(bf16[69,64,128]{0,2,1:T(8,128)(2,1)S(1)} %get-tuple-element.3) | copy-start | bytes 3391492
  149.9 225.8 %all-reduce.2.cloned.1.call-start = ((), (), s32[]{:S(2)}) async-start(), calls=%async_computation.5 | async-start | bytes 589824 | tf_op jit(solution)/shard_map/psum | solution.py:117
  150.0 2.3 copy-start.8
  152.2 1.6 copy-start.6
  153.8 1.3 copy-start.13
  153.8 1.7 copy-start.9
  155.1 1.4 copy-start.11
  155.6 1.7 copy-start.3
  157.3 1.6 copy-start.1
  159.8 0.7 copy-start.16
  160.6 713.4 %reduce-scatter.5.cloned.1.call-start = ((), (), s32[]{:S(2)}) async-start(), calls=%async_computation.6 | async-start | bytes 4227072 | tf_op jit(solution)/shard_map/reduce_scatter | solution.py:107
Sparse Core Ops, SparseCore 0:
  150.0 14.0 reduce-scatter.2
  171.1 702.7 reduce-scatter.4
Sparse Core Ops, SparseCore 1:
  160.7 215.0 all-reduce.1
where the time goes:
time: 893 us; the launch traced here: 884 us
  waiting for transfers between devices  678 us (76%)
  local copies, waits for them, and re-layouts  86.6 us (10%)
  matrix products  40.4 us (5%)
  blocking collectives  23.6 us (3%)
  starting transfers between devices  21.5 us (2%)
  other arithmetic  17.8 us (2%)
  between operations  16.1 us (2%)
    reduce_scatter x1, waiting for transfers between devices, body(): lax.psum_scatter(embed_terms.reshape(local_channels, 16 * width), ('lon',...  498 us
    psum x1, waiting for transfers between devices, body(): conv_gradient = lax.psum(conv_terms, ('lon', 'lat'))  180 us
    unnamed x48, local copies, waits for them, and re-layouts  24 us
    all_to_all x1, blocking collectives, body(): lax.all_to_all(embedded, 'lon', split_axis=0, concat_axis=1, tiled=True)  23.6 us
    dot_general x9, matrix products, convolve(): jnp.dot(weights[:, position, :], window.reshape(extended.shape[0], row_co...  19.7 us
  transfers between devices with their start and end apart: 10, of which 2 were waited for; matrix products, arithmetic and copies ran while one was open for 8% of the time, Pallas kernels for 0%

commit v1 on v0

v1 whole, which is shorter than its diff:
```python
import functools

import jax
import jax.numpy as jnp
from jax import lax
from jax.experimental import pallas as pl
from jax.experimental.pallas import tpu as pltpu
from jax.sharding import PartitionSpec as P

BF = jnp.bfloat16
F32 = jnp.float32
MESH = pl.DeviceIdType.MESH
CP = 80
NN = (((1,), (0,)), ((), ()))
NT = (((1,), (1,)), ((), ()))


def dot(x, y, dims=NN):
    return lax.dot_general(x, y, dims, preferred_element_type=F32)


def one_hot(target, rows):
    index = lax.broadcasted_iota(jnp.int32, (rows, target.shape[1]), 0)
    return jnp.where(index == target, 1.0, 0.0).astype(BF)


def kernel(
    t_ref, wc_ref, w_ref, tg_ref,
    emb_out, eg_out, cg_out,
    slab, halo_l, halo_r, got_l, got_r, pack_l, pack_r,
    wc, wv, tgo, tgp, src, p1, xs, hid, hidp, hidt, dgelu, emb,
    egb, ego, ra, sbf, sbb, rb, scf, scb, rc,
    cga, cgp, scg, rcg, l0, rl, l1, agb, full,
    loc, tg_s, tg_r, ha_s, ha_r, pk_s, pk_r, wc_s, wc_r, em_s, em_r, tf_s, tf_r, hp_s, hp_r,
    a_s, a_r, b_s, b_r, c_s, c_r, q_s, q_r, d_s, d_r, e_s, e_r, f_s, f_r,
):
    lon = lax.axis_index("lon")
    lat = lax.axis_index("lat")
    ch = lax.axis_index("ch")
    hi = lon // 8
    lo = lax.rem(lon, 8)
    y = lat // 2
    xlo = lax.rem(lat, 2)
    other = 1 - ch

    def remote(source, target, send, recv, to_lon, to_lat, to_ch):
        return pltpu.make_async_remote_copy(
            src_ref=source, dst_ref=target, send_sem=send, recv_sem=recv,
            device_id=(to_lon, to_lat, to_ch), device_id_type=MESH,
        )

    slab_copy = pltpu.make_async_copy(t_ref.at[pl.ds(31 * ch, 33)], slab.at[pl.ds(other, 33)], loc.at[0])
    slab_copy.start()

    def halo_copies(row, to_lat, base):
        out = []
        for n, (shift, target) in enumerate(((0, slab.at[33 * ch]), (1, halo_l), (15, halo_r))):
            to = lax.rem(base + shift, 16)
            out.append(remote(t_ref.at[row], target, ha_s.at[n], ha_r.at[n], to, to_lat, ch))
        return out

    inner = halo_copies(63 * other, lat + 1 - 2 * ch, lon)
    polar_s = []
    for n, (shift, target) in enumerate(((0, slab.at[33 * ch]), (1, halo_l), (15, halo_r))):
        to = lax.rem(lon + 8 + shift, 16)
        polar_s.append(remote(t_ref.at[63 * ch], target, ha_s.at[3 + n], ha_r.at[n], to, lat, ch))
    has_inner = lat != 7 * other
    has_polar = lat == 7 * ch

    @pl.when(has_inner)
    def _():
        for c in inner:
            c.start()

    @pl.when(has_polar)
    def _():
        for c in polar_s:
            c.start()

    wc_local = pltpu.make_async_copy(wc_ref, wc.at[:, pl.ds(pl.multiple_of(64 * ch, 64), 64), :], loc.at[1])
    wc_local.start()
    wc_remote = remote(
        wc_ref, wc.at[:, pl.ds(pl.multiple_of(64 * ch, 64), 64), :], wc_s, wc_r, lon, lat, other
    )
    wc_remote.start()

    tg_copies = []
    for i in range(8):
        to = 8 * ch + lax.rem(lo + i, 8)
        tg_copies.append(
            remote(
                tg_ref.at[pl.ds(pl.multiple_of(32 * to, 32), 32)],
                tgo.at[pl.ds(pl.multiple_of(32 * lo, 32), 32)],
                tg_s.at[i], tg_r.at[i], to, lat, hi,
            )
        )
    tg_self = pltpu.make_async_copy(
        tg_ref.at[pl.ds(pl.multiple_of(32 * lon, 32), 32)],
        tgo.at[pl.ds(pl.multiple_of(32 * lo, 32), 32)],
        tg_r.at[0],
    )

    for i in (4, 3, 5, 2, 6, 1, 7):
        tg_copies[i].start()

    @pl.when(ch == hi)
    def _():
        tg_self.start()

    @pl.when(ch != hi)
    def _():
        tg_copies[0].start()

    w_copies = [
        pltpu.make_async_copy(w_ref.at[:, pl.ds(1024 * s, 1024)], wv.at[s], loc.at[2 + s]) for s in range(16)
    ]
    for c in w_copies:
        c.start()

    j = lax.broadcasted_iota(jnp.int32, (1, 768), 1)
    column = 4 * (j % 32) + j // 128 - 1
    target = jnp.where((column >= 0) & (column < 128), column + 128 * ((j % 128) // 32), -1)
    p1[...] = one_hot(target, 512)
    xs[:, 480:496, :] = jnp.zeros((6, 16, 256), BF)
    cga[...] = jnp.zeros_like(cga)

    slab_copy.wait()
    lane = lax.broadcasted_iota(jnp.int32, (CP, 128), 1)
    left = jnp.zeros((CP, 128), F32)
    right = jnp.zeros((CP, 128), F32)
    for m in range(33):
        row = slab[other + m].astype(F32)
        if m:
            row = pltpu.roll(row, m, 1)
        left = jnp.where(lane == (m + 127) % 128, row, left)
        right = jnp.where(lane == m, row, right)
    pack_l[...] = left.astype(BF)
    pack_r[...] = right.astype(BF)
    pk0 = remote(pack_l, got_l, pk_s.at[0], pk_r.at[0], lax.rem(lon + 1, 16), lat, ch)
    pk1 = remote(pack_r, got_r, pk_s.at[1], pk_r.at[1], lax.rem(lon + 15, 16), lat, ch)
    pk0.start()
    pk1.start()

    for c in inner:
        c.wait_recv()

    def gather_rows(u, _):
        for half in range(2):
            for k in range(4):
                src[u, pl.ds(CP * half, CP), 128 * k : 128 * k + 128] = slab[16 * half + 4 * k + u]
        return 0

    lax.fori_loop(0, 6, gather_rows, 0)
    pk0.wait_recv()
    pk1.wait_recv()
    edges = jnp.concatenate([got_l[...], got_r[...], halo_l[...], halo_r[...]], axis=1)
    j2 = lax.broadcasted_iota(jnp.int32, (1, 256), 1)
    side = j2 // 128
    at_edge = (j2 % 32) == 31 * side

    def depth(u, _):
        res = dot(src[u], p1[...])
        for half in range(2):
            row = 16 * half + u + 4 * ((j2 % 128) // 32)
            m = row - other
            own = jnp.where(side == 0, (m + 127) % 128, 128 + m)
            want = jnp.where(row == 33 * ch, jnp.where(side == 0, 256 + 127, 384), own)
            fill = dot(edges, one_hot(jnp.where(at_edge, want, -1), 512))
            part = res[CP * half : CP * half + CP]
            lanes = slice(128 * half, 128 * half + 128)
            xs[u, 0:CP, lanes] = (part[:, 0:128] + fill[:, 0:128]).astype(BF)
            for v in range(1, 5):
                xs[u, CP * v : CP * v + CP, lanes] = part[:, 128 * v : 128 * v + 128].astype(BF)
            xs[u, CP * 5 : CP * 6, lanes] = (part[:, 640:768] + fill[:, 128:256]).astype(BF)
        return 0

    lax.fori_loop(0, 6, depth, 0)

    wc_local.wait()
    wc_remote.wait_recv()

    def conv(s, _):
        a = s // 4
        first = pl.multiple_of(CP * (s % 4), 16)
        v = jnp.zeros((128, 256), F32)
        for da in range(3):
            v = v + dot(wc[da], xs[a + da, pl.ds(first, 256), :])
        root = 0.7978845608028654
        square = v * v
        th = jnp.tanh(root * v * (1.0 + 0.044715 * square))
        half = 0.5 * (1.0 + th)
        slope = half + 0.5 * v * (1.0 - th * th) * (root * (1.0 + 3 * 0.044715 * square))
        h = (v * half).astype(BF)
        dgelu[s] = slope
        hid[s] = h.reshape(2, 64, 256)
        hidt[:, pl.ds(pl.multiple_of(128 * s, 128), 128)] = h.T
        return 0

    lax.fori_loop(0, 16, conv, 0)
    hp = remote(hid.at[:, other], hidp, hp_s, hp_r, lon, lat, other)
    hp.start()

    for c in w_copies:
        c.wait()

    def embed(n, _):
        columns = pl.ds(pl.multiple_of(256 * n, 256), 256)
        part = jnp.zeros((256, 256), F32)
        for s in range(16):
            part = part + dot(hidt[:, 128 * s : 128 * s + 128], wv[s, :, columns])
        emb[n // 2, :, pl.ds(pl.multiple_of(256 * (n % 2), 256), 256)] = part.astype(BF)
        return 0

    lax.fori_loop(0, 4, embed, 0)
    emb_copies = {}
    for i in (4, 3, 5, 2, 6, 1, 7, 0):
        r = lax.rem(lo + i, 8)
        for g in range(2):
            emb_copies[i, g] = remote(
                emb.at[g, pl.ds(pl.multiple_of(32 * r, 32), 32)],
                emb_out.at[pl.ds(pl.multiple_of(32 * lon, 32), 32)],
                em_s.at[2 * i + g], em_r.at[2 * i + hi], 8 * ch + r, lat, g,
            )
            if i:
                emb_copies[i, g].start()
            else:
                mine = (ch == hi) & (ch == g)

                @pl.when(mine)
                def _(g=g):
                    pltpu.make_async_copy(
                        emb.at[g, pl.ds(pl.multiple_of(32 * lo, 32), 32)],
                        emb_out.at[pl.ds(pl.multiple_of(32 * lon, 32), 32)],
                        em_r.at[hi],
                    ).start()

                @pl.when(jnp.logical_not(mine))
                def _(g=g):
                    emb_copies[0, g].start()

    forwards = []
    for n, i in enumerate((0, 1, 7, 2, 6, 3, 5, 4)):
        tg_copies[i].wait_recv()
        rows = pl.ds(pl.multiple_of(32 * lax.rem(lo + 8 - i, 8), 32), 32)
        c = remote(tgo.at[rows], tgp.at[rows], tf_s.at[n], tf_r.at[n], lon, lat, other)
        c.start()
        forwards.append(c)
    hp.wait_recv()
    for c in forwards:
        c.wait_recv()

    def a_copy(cc, n):
        rows = pl.ds(pl.multiple_of(256 * cc, 256), 256)
        return remote(
            egb.at[n - 1, rows], ra.at[n - 1, rows], a_s.at[cc, n - 1], a_r.at[cc, n - 1],
            lon, lax.rem(lat + 2 * n, 8), ch,
        )

    def eg_part(cc, n):
        columns = pl.ds(pl.multiple_of(256 * lax.rem(y + n, 4), 256), 256)
        mine = hid[pl.ds(4 * cc, 4), ch].reshape(256, 256)
        theirs = hidp[pl.ds(4 * cc, 4)].reshape(256, 256)
        return dot(mine, tgo[:, columns]) + dot(theirs, tgp[:, columns])

    def stage_a(cc, _):
        rows = pl.ds(pl.multiple_of(256 * cc, 256), 256)
        for n in (2, 1, 3):
            egb[n - 1, rows] = eg_part(cc, n).astype(BF)
            a_copy(cc, n).start()
        ego[rows] = eg_part(cc, 0)
        return 0

    lax.fori_loop(0, 4, stage_a, 0)

    def conv_grad(a, _):
        hg = dot(wv[pl.ds(4 * a, 4)].reshape(512, 1024), tgo[...], NT)
        pg = (hg * dgelu[pl.ds(4 * a, 4)].reshape(512, 256)).astype(BF)
        for b in range(4):
            for da in range(3):
                cga[da] += dot(pg[128 * b : 128 * b + 128], xs[a + da, CP * b : CP * b + 256, :], NT)
        return 0

    lax.fori_loop(0, 4, conv_grad, 0)
    theirs = pl.ds(pl.multiple_of(64 * other, 64), 64)
    q_copy = remote(cga.at[:, theirs, :], cgp, q_s, q_r, lon, lat, other)
    q_copy.start()

    def b_copy(cc):
        rows = pl.ds(pl.multiple_of(256 * cc, 256), 256)
        return remote(sbb.at[other_x, rows], rb.at[rows], b_s.at[cc], b_r.at[cc], lon, lat + 1 - 2 * xlo, ch)

    other_x = 1 - xlo

    def stage_b(cc, _):
        rows = pl.ds(pl.multiple_of(256 * cc, 256), 256)
        total = ego[rows]
        for n in (1, 3, 2):
            a_copy(cc, n).wait_recv()
            total = total + ra[n - 1, rows].astype(F32)
        for g in range(2):
            piece = total[:, 128 * g : 128 * g + 128]
            sbf[g, rows] = piece
            sbb[g, rows] = piece.astype(BF)
        b_copy(cc).start()
        return 0

    def c_copy(s):
        i = lax.rem(s - lon + 16, 16)
        return remote(scb.at[s], rc.at[i], c_s.at[i], c_r.at[i], s, lat, ch)

    def stage_c(cc, _):
        rows = pl.ds(pl.multiple_of(256 * cc, 256), 256)
        b_copy(cc).wait_recv()
        total = (sbf[xlo, rows] + rb[rows].astype(F32)).reshape(4, 64, 128)
        scf[pl.ds(4 * cc, 4)] = total
        scb[pl.ds(4 * cc, 4)] = total.astype(BF)
        for k in range(4):
            s = 4 * cc + k

            @pl.when(s != lon)
            def _():
                c_copy(s).start()

        return 0

    def d_copy(i):
        to = lax.rem(lon + i, 16)
        return remote(scg.at[to], rcg.at[i], d_s.at[i], d_r.at[i], to, lat, ch)

    def e_copy(i):
        return remote(l0, rl.at[lat], e_s.at[i], e_r.at[i], lon, lax.rem(lat + i, 8), ch)

    def f_copy(i):
        return remote(l1, agb.at[lon], f_s.at[i], f_r.at[i], lax.rem(lon + i, 16), lat, ch)

    q_copy.wait_recv()
    total = cga[:, pl.ds(pl.multiple_of(64 * ch, 64), 64), :] + cgp[...]
    for n in range(16):
        ob, half = n // 2, n % 2
        scg[n] = total[:, 8 * ob : 8 * ob + 8, 128 * half : 128 * half + 128]
    for i in range(1, 16):
        d_copy(i).start()

    stage_b(0, 0)

    total = scg[lon]
    for i in range(1, 16):
        d_copy(i).wait_recv()
        total = total + rcg[i]
    l0[...] = total
    rl[lat] = total
    for i in range(1, 8):
        e_copy(i).start()

    stage_b(1, 0)
    stage_c(0, 0)

    for i in range(1, 8):
        e_copy(i).wait_recv()
    total = rl[0]
    for i in range(1, 8):
        total = total + rl[i]
    l1[...] = total
    agb[lon] = total
    for i in range(1, 16):
        f_copy(i).start()

    stage_b(2, 0)
    stage_c(1, 0)
    stage_b(3, 0)
    stage_c(2, 0)

    for i in range(1, 16):
        f_copy(i).wait_recv()
    for n in range(16):
        ob, half = n // 2, n % 2
        full[:, 8 * ob : 8 * ob + 8, 128 * half : 128 * half + 128] = agb[n]
    for da in range(3):
        for db in range(3):
            cg_out[3 * da + db] = full[da, :, CP * db : CP * db + 69]

    stage_c(3, 0)
    total = scf[lon]
    for i in range(1, 16):
        remote(scb.at[0], rc.at[i], c_s.at[i], c_r.at[i], lon, lat, other).wait_recv()
        total = total + rc[i].astype(F32)
    eg_out[...] = total

    for i in range(8):
        for g in range(2):
            remote(
                emb.at[0, pl.ds(0, 32)], emb_out.at[pl.ds(0, 32)],
                em_s.at[0], em_r.at[2 * i + g], lon, lat, other,
            ).wait_recv()

    @pl.when(has_inner)
    def _():
        for c in inner:
            c.wait_send()

    @pl.when(has_polar)
    def _():
        for c in polar_s:
            c.wait_send()

    wc_remote.wait_send()
    for i in range(1, 8):
        tg_copies[i].wait_send()

    @pl.when(ch != hi)
    def _():
        tg_copies[0].wait_send()

    pk0.wait_send()
    pk1.wait_send()
    hp.wait_send()
    q_copy.wait_send()
    for c in forwards:
        c.wait_send()
    for (i, g), c in emb_copies.items():
        if i:
            c.wait_send()
        else:

            @pl.when(jnp.logical_not((ch == hi) & (ch == g)))
            def _(c=c):
                c.wait_send()

    for cc in range(4):
        for n in (1, 2, 3):
            a_copy(cc, n).wait_send()
        b_copy(cc).wait_send()
    for i in range(1, 16):
        remote(scb.at[0], rc.at[i], c_s.at[i], c_r.at[i], lon, lat, other).wait_send()
        d_copy(i).wait_send()
        f_copy(i).wait_send()
    for i in range(1, 8):
        e_copy(i).wait_send()


def step(t, wc, w, tg):
    vm = pltpu.VMEM
    sem = pltpu.SemaphoreType.DMA
    scratch = [
        vm((34, CP, 128), BF), vm((CP, 128), BF), vm((CP, 128), BF), vm((CP, 128), BF), vm((CP, 128), BF),
        vm((CP, 128), BF), vm((CP, 128), BF),
        vm((3, 128, 256), BF), vm((16, 128, 1024), BF), vm((256, 1024), BF), vm((256, 1024), BF),
        vm((6, 2 * CP, 512), BF), vm((512, 768), BF), vm((6, 496, 256), BF),
        vm((16, 2, 64, 256), BF), vm((16, 64, 256), BF), vm((256, 2048), BF), vm((16, 128, 256), F32),
        vm((2, 256, 512), BF),
        vm((3, 1024, 256), BF), vm((1024, 256), F32), vm((3, 1024, 256), BF),
        vm((2, 1024, 128), F32), vm((2, 1024, 128), BF), vm((1024, 128), BF),
        vm((16, 64, 128), F32), vm((16, 64, 128), BF), vm((16, 64, 128), BF),
        vm((3, 128, 256), F32), vm((3, 64, 256), F32), vm((16, 3, 8, 128), F32), vm((16, 3, 8, 128), F32),
        vm((3, 8, 128), F32), vm((8, 3, 8, 128), F32), vm((3, 8, 128), F32), vm((16, 3, 8, 128), F32),
        vm((3, 64, 256), F32),
        sem((18,)), sem((8,)), sem((8,)), sem((6,)), sem((3,)), sem((2,)), sem((2,)), sem, sem,
        sem((16,)), sem((16,)), sem((8,)), sem((8,)), sem, sem,
        sem((4, 3)), sem((4, 3)), sem((4,)), sem((4,)), sem((16,)), sem((16,)), sem, sem,
        sem((16,)), sem((16,)), sem((8,)), sem((8,)), sem((16,)), sem((16,)),
    ]
    any_ = pl.BlockSpec(memory_space=pl.ANY)
    inside = pl.BlockSpec(memory_space=pltpu.VMEM)
    return pl.pallas_call(
        kernel,
        out_shape=(
            jax.ShapeDtypeStruct((512, 512), BF),
            jax.ShapeDtypeStruct((64, 128), F32),
            jax.ShapeDtypeStruct((9, 64, 69), F32),
        ),
        in_specs=[any_] * 4,
        out_specs=(any_, inside, inside),
        scratch_shapes=scratch,
        compiler_params=pltpu.CompilerParams(vmem_limit_bytes=56 * 1024 * 1024, has_side_effects=True),
    )(t, wc, w, tg)


def body(fields, conv_weight, embed_weight, token_grads):
    t = jnp.pad(fields.transpose(1, 0, 2), ((0, 0), (0, CP - 69), (0, 0)))
    wc = jnp.pad(conv_weight.reshape(64, 3, 3, 69), ((0, 0), (0, 0), (0, 0), (0, CP - 69)))
    wc = jnp.pad(wc.reshape(64, 3, 3 * CP), ((0, 0), (0, 0), (0, 16))).transpose(1, 0, 2)
    embedded, embed_gradient, conv_gradient = step(t, wc, embed_weight, token_grads.reshape(512, 1024))
    return embedded.reshape(1, 1, 512, 512), conv_gradient.transpose(1, 0, 2), embed_gradient


def solution(mesh):
    return jax.shard_map(
        body,
        mesh=mesh,
        in_specs=(P(None, "lat", "lon"), P("ch", None, None), P(), P("lon", "lat", None, None)),
        out_specs=(P("lon", "lat", None, "ch"), P("ch", None, None), P("ch", ("lon", "lat"))),
        check_vma=False,
    )
```

time: 893 us -> 95.2 us (0.11)
  the two profiles are of different devices: /device:TPU:0 before, /device:TPU:1 now
where the time goes in v1:
time: 95.2 us; the launch traced here: 94.8 us
  Pallas kernels  85.7 us (90%)
  local copies, waits for them, and re-layouts  8.38 us (9%)
    pallas_call x1, Pallas kernels, step(): pl.pallas_call(kernel, out_shape=(jax.ShapeDtypeStruct((512, 512), BF), j...  85.7 us
    unnamed x8, local copies, waits for them, and re-layouts  6.18 us

profile of v1, /device:TPU:1, one launch (start us, length us, event | category | flops | bytes accessed | tf_op | source)
XLA Modules:
  0.0 94.8 jit_solution(8442478705215702501)
XLA Ops:
  0.6 2.0 %copy.12 = bf16[69,64,128]{2,0,1:T(8,128)(2,1)S(1)} copy(bf16[69,64,128]{2,1,0:T(8,128)(2,1)} %param.4) | data formatting | bytes 2260992 | tf_op args[0]
  2.6 0.0 copy-start
  2.6 1.2 %pad.12.t_ref = bf16[64,80,128]{2,1,0:T(8,128)(2,1)} pad(bf16[64,69,128]{2,1,0:T(8,128)(2,1)S(1)} %bitcast.11, bf16[]{:T(256)} %constant.2.clone.1), padding=0_0x0_11x0_0 | pad | bytes 2441218 | tf_op jit(solution)/shard_map/jit(_pad)/pad | solution.py:479
  3.8 0.0 copy-done
  3.8 0.1 copy.10
  3.9 0.1 pad.13
  4.0 0.1 reshape.19
  4.2 0.7 pad_bitcast_fusion.wc_ref
  4.9 85.7 %shard_map.67 = (bf16[512,512]{1,0:T(8,128)(2,1)}, f32[64,128]{1,0:T(8,128)}, f32[9,64,69]{2,1,0:T(8,128)}) custom-call(bf16[64,80,128]{2,1,0:T(8,128)(2,1)} %pad.12.t_ref, bf16[3,64,256]{2,1,0:T(8,128)(2,1)} %pad_bitcast_fusion.wc_ref, bf16[128,16384]{1,0:T(8,128)(2,1)} %w_ref.1, bf16[512,1024]{1,0:T(8,128)(2,1)} %bitcast.12), custom_call_target="tpu_custom_call" | custom-call | tf_op jit(solution)/shard_map/pallas_call | solution.py:464
  90.6 0.0 copy-start.1
  90.6 1.9 %copy.16 = bf16[1,1,512,512]{3,2,1,0:T(8,128)(2,1)} copy(bf16[1,1,512,512]{3,2,1,0:T(8,128)(2,1)} %bitcast.13) | data formatting | bytes 1048576
  92.5 1.7 %copy.17 = f32[64,9,69]{2,0,1:T(8,128)} copy(f32[64,9,69]{2,0,1:T(8,128)} %bitcast.14) | data formatting | bytes 317952
  94.1 0.0 copy-done.1
  94.1 0.6 copy.18
Async XLA Ops:
  2.6 1.2 %copy-start = (bf16[64,9,69]{2,0,1:T(8,128)(2,1)S(1)}, bf16[64,9,69]{2,0,1:T(8,128)(2,1)}, u32[]{:S(2)}) copy-start(bf16[64,9,69]{2,0,1:T(8,128)(2,1)} %param.5) | copy-start | bytes 238468
  90.6 3.6 %copy-start.1 = (f32[64,128]{1,0:T(8,128)S(1)}, f32[64,128]{1,0:T(8,128)}, u32[]{:S(2)}) copy-start(f32[64,128]{1,0:T(8,128)} %get-tuple-element.14) | copy-start | bytes 98308

commit v2 on v1

--- a/solution.py
+++ b/solution.py
@@ -49,68 +49,38 @@
             device_id=(to_lon, to_lat, to_ch), device_id_type=MESH,
         )
 
+    barrier = pltpu.get_barrier_semaphore()
+
+    def greet(to_lon, to_lat, to_ch):
+        pl.semaphore_signal(barrier, inc=1, device_id=(to_lon, to_lat, to_ch), device_id_type=MESH)
+
+    for i in range(1, 16):
+        greet(lax.rem(lon + i, 16), lat, ch)
+        greet(lax.rem(lon + i, 16), lat, other)
+    greet(lon, lat, other)
+    for i in range(1, 8):
+        greet(lon, lax.rem(lat + i, 8), ch)
+
+    @pl.when(lat > 0)
+    def _():
+        greet(lax.rem(lon + 1, 16), lat - 1, ch)
+        greet(lax.rem(lon + 15, 16), lat - 1, ch)
+
+    @pl.when(lat < 7)
+    def _():
+        greet(lax.rem(lon + 1, 16), lat + 1, ch)
+        greet(lax.rem(lon + 15, 16), lat + 1, ch)
+
     slab_copy = pltpu.make_async_copy(t_ref.at[pl.ds(31 * ch, 33)], slab.at[pl.ds(other, 33)], loc.at[0])
     slab_copy.start()
 
-    def halo_copies(row, to_lat, base):
-        out = []
-        for n, (shift, target) in enumerate(((0, slab.at[33 * ch]), (1, halo_l), (15, halo_r))):
-            to = lax.rem(base + shift, 16)
-            out.append(remote(t_ref.at[row], target, ha_s.at[n], ha_r.at[n], to, to_lat, ch))
-        return out
-
-    inner = halo_copies(63 * other, lat + 1 - 2 * ch, lon)
-    polar_s = []
-    for n, (shift, target) in enumerate(((0, slab.at[33 * ch]), (1, halo_l), (15, halo_r))):
-        to = lax.rem(lon + 8 + shift, 16)
-        polar_s.append(remote(t_ref.at[63 * ch], target, ha_s.at[3 + n], ha_r.at[n], to, lat, ch))
-    has_inner = lat != 7 * other
-    has_polar = lat == 7 * ch
-
-    @pl.when(has_inner)
-    def _():
-        for c in inner:
-            c.start()
-
-    @pl.when(has_polar)
-    def _():
-        for c in polar_s:
-            c.start()
-
-    wc_local = pltpu.make_async_copy(wc_ref, wc.at[:, pl.ds(pl.multiple_of(64 * ch, 64), 64), :], loc.at[1])
-    wc_local.start()
-    wc_remote = remote(
-        wc_ref, wc.at[:, pl.ds(pl.multiple_of(64 * ch, 64), 64), :], wc_s, wc_r, lon, lat, other
-    )
-    wc_remote.start()
-
-    tg_copies = []
-    for i in range(8):
-        to = 8 * ch + lax.rem(lo + i, 8)
-        tg_copies.append(
-            remote(
-                tg_ref.at[pl.ds(pl.multiple_of(32 * to, 32), 32)],
-                tgo.at[pl.ds(pl.multiple_of(32 * lo, 32), 32)],
-                tg_s.at[i], tg_r.at[i], to, lat, hi,
-            )
-        )
-    tg_self = pltpu.make_async_copy(
-        tg_ref.at[pl.ds(pl.multiple_of(32 * lon, 32), 32)],
-        tgo.at[pl.ds(pl.multiple_of(32 * lo, 32), 32)],
-        tg_r.at[0],
-    )
-
-    for i in (4, 3, 5, 2, 6, 1, 7):
-        tg_copies[i].start()
-
-    @pl.when(ch == hi)
-    def _():
-        tg_self.start()
-
-    @pl.when(ch != hi)
-    def _():
-        tg_copies[0].start()
-
+    own_half = pl.ds(pl.multiple_of(64 * ch, 64), 64)
+    for da in range(3):
+        gap = jnp.zeros((64, CP - 69), F32)
+        parts = []
+        for db in range(3):
+            parts += [wc_ref[3 * da + db].astype(F32), gap]
+        wc[da, own_half] = jnp.concatenate(parts + [jnp.zeros((64, 16), F32)], axis=1).astype(BF)
     w_copies = [
         pltpu.make_async_copy(w_ref.at[:, pl.ds(1024 * s, 1024)], wv.at[s], loc.at[2 + s]) for s in range(16)
     ]
@@ -136,10 +106,70 @@
         right = jnp.where(lane == m, row, right)
     pack_l[...] = left.astype(BF)
     pack_r[...] = right.astype(BF)
+    @pl.when((lat == 0) | (lat == 7))
+    def _():
+        pl.semaphore_wait(barrier, 40)
+
+    @pl.when((lat > 0) & (lat < 7))
+    def _():
+        pl.semaphore_wait(barrier, 42)
+
+    def halo_copies(row, to_lat, base):
+        out = []
+        for n, (shift, target) in enumerate(((0, slab.at[33 * ch]), (1, halo_l), (15, halo_r))):
+            to = lax.rem(base + shift, 16)
+            out.append(remote(t_ref.at[row], target, ha_s.at[n], ha_r.at[n], to, to_lat, ch))
+        return out
+
+    inner = halo_copies(63 * other, lat + 1 - 2 * ch, lon)
+    polar_s = []
+    for n, (shift, target) in enumerate(((0, slab.at[33 * ch]), (1, halo_l), (15, halo_r))):
+        to = lax.rem(lon + 8 + shift, 16)
+        polar_s.append(remote(t_ref.at[63 * ch], target, ha_s.at[3 + n], ha_r.at[n], to, lat, ch))
+    has_inner = lat != 7 * other
+    has_polar = lat == 7 * ch
+
+    @pl.when(has_inner)
+    def _():
+        for c in inner:
+            c.start()
+
+    @pl.when(has_polar)
+    def _():
+        for c in polar_s:
+            c.start()
+
     pk0 = remote(pack_l, got_l, pk_s.at[0], pk_r.at[0], lax.rem(lon + 1, 16), lat, ch)
     pk1 = remote(pack_r, got_r, pk_s.at[1], pk_r.at[1], lax.rem(lon + 15, 16), lat, ch)
     pk0.start()
     pk1.start()
+
+    wc_remote = remote(wc.at[:, own_half], wc.at[:, own_half], wc_s, wc_r, lon, lat, other)
+    wc_remote.start()
+
+    order = (2, 1, 3, 0)
+    tg_copies = {}
+    for n in order:
+        columns = pl.ds(pl.multiple_of(256 * lax.rem(y + n, 4), 256), 256)
+        for i in (4, 3, 5, 2, 6, 1, 7, 0):
+            to = 8 * ch + lax.rem(lo + i, 8)
+            rows = pl.ds(pl.multiple_of(32 * to, 32), 32)
+            place = pl.ds(pl.multiple_of(32 * lo, 32), 32)
+            c = remote(
+                tg_ref.at[rows, columns], tgo.at[place, columns], tg_s.at[n, i], tg_r.at[n, i], to, lat, hi,
+            )
+            tg_copies[n, i] = c
+            if i:
+                c.start()
+            else:
+
+                @pl.when(ch == hi)
+                def _():
+                    pltpu.make_async_copy(tg_ref.at[rows, columns], tgo.at[place, columns], tg_r.at[n, 0]).start()
+
+                @pl.when(ch != hi)
+                def _():
+                    c.start()
 
     for c in inner:
         c.wait_recv()
@@ -176,7 +206,6 @@
 
     lax.fori_loop(0, 6, depth, 0)
 
-    wc_local.wait()
     wc_remote.wait_recv()
 
     def conv(s, _):
@@ -238,17 +267,6 @@
                 def _(g=g):
                     emb_copies[0, g].start()
 
-    forwards = []
-    for n, i in enumerate((0, 1, 7, 2, 6, 3, 5, 4)):
-        tg_copies[i].wait_recv()
-        rows = pl.ds(pl.multiple_of(32 * lax.rem(lo + 8 - i, 8), 32), 32)
-        c = remote(tgo.at[rows], tgp.at[rows], tf_s.at[n], tf_r.at[n], lon, lat, other)
-        c.start()
-        forwards.append(c)
-    hp.wait_recv()
-    for c in forwards:
-        c.wait_recv()
-
     def a_copy(cc, n):
         rows = pl.ds(pl.multiple_of(256 * cc, 256), 256)
         return remote(
@@ -262,15 +280,29 @@
         theirs = hidp[pl.ds(4 * cc, 4)].reshape(256, 256)
         return dot(mine, tgo[:, columns]) + dot(theirs, tgp[:, columns])
 
-    def stage_a(cc, _):
-        rows = pl.ds(pl.multiple_of(256 * cc, 256), 256)
-        for n in (2, 1, 3):
-            egb[n - 1, rows] = eg_part(cc, n).astype(BF)
-            a_copy(cc, n).start()
-        ego[rows] = eg_part(cc, 0)
-        return 0
-
-    lax.fori_loop(0, 4, stage_a, 0)
+    forwards = []
+    for n in order:
+        for i in range(8):
+            tg_copies[n, i].wait_recv()
+        columns = pl.ds(pl.multiple_of(256 * lax.rem(y + n, 4), 256), 256)
+        c = remote(tgo.at[:, columns], tgp.at[:, columns], tf_s.at[n], tf_r.at[n], lon, lat, other)
+        c.start()
+        forwards.append(c)
+        if n == 2:
+            hp.wait_recv()
+        c.wait_recv()
+
+        def stage_a(cc, _, n=n):
+            rows = pl.ds(pl.multiple_of(256 * cc, 256), 256)
+            if n:
+                egb[n - 1, rows] = eg_part(cc, n).astype(BF)
+                a_copy(cc, n).start()
+            else:
+                ego[rows] = eg_part(cc, 0)
+            return 0
+
+        lax.fori_loop(0, 4, stage_a, 0)
+
 
     def conv_grad(a, _):
         hg = dot(wv[pl.ds(4 * a, 4)].reshape(512, 1024), tgo[...], NT)
@@ -404,12 +436,14 @@
             c.wait_send()
 
     wc_remote.wait_send()
-    for i in range(1, 8):
-        tg_copies[i].wait_send()
+    for n in order:
+        for i in range(1, 8):
+            tg_copies[n, i].wait_send()
 
     @pl.when(ch != hi)
     def _():
-        tg_copies[0].wait_send()
+        for n in order:
+            tg_copies[n, 0].wait_send()
 
     pk0.wait_send()
     pk1.wait_send()
@@ -454,8 +488,8 @@
         vm((3, 128, 256), F32), vm((3, 64, 256), F32), vm((16, 3, 8, 128), F32), vm((16, 3, 8, 128), F32),
         vm((3, 8, 128), F32), vm((8, 3, 8, 128), F32), vm((3, 8, 128), F32), vm((16, 3, 8, 128), F32),
         vm((3, 64, 256), F32),
-        sem((18,)), sem((8,)), sem((8,)), sem((6,)), sem((3,)), sem((2,)), sem((2,)), sem, sem,
-        sem((16,)), sem((16,)), sem((8,)), sem((8,)), sem, sem,
+        sem((18,)), sem((4, 8)), sem((4, 8)), sem((6,)), sem((3,)), sem((2,)), sem((2,)), sem, sem,
+        sem((16,)), sem((16,)), sem((4,)), sem((4,)), sem, sem,
         sem((4, 3)), sem((4, 3)), sem((4,)), sem((4,)), sem((16,)), sem((16,)), sem, sem,
         sem((16,)), sem((16,)), sem((8,)), sem((8,)), sem((16,)), sem((16,)),
     ]
@@ -468,18 +502,37 @@
             jax.ShapeDtypeStruct((64, 128), F32),
             jax.ShapeDtypeStruct((9, 64, 69), F32),
         ),
-        in_specs=[any_] * 4,
+        in_specs=[any_, inside, any_, any_],
         out_specs=(any_, inside, inside),
         scratch_shapes=scratch,
-        compiler_params=pltpu.CompilerParams(vmem_limit_bytes=56 * 1024 * 1024, has_side_effects=True),
+        compiler_params=pltpu.CompilerParams(vmem_limit_bytes=56 * 1024 * 1024, has_side_effects=True, collective_id=0),
     )(t, wc, w, tg)
+
+
+def settle(emb, eg, cg, emb_out, eg_out, cg_out):
+    emb_out[...] = emb[...]
+
+    @pl.when(pl.program_id(0) == 0)
+    def _():
+        eg_out[...] = eg[...]
+        cg_out[...] = cg[...]
 
 
 def body(fields, conv_weight, embed_weight, token_grads):
     t = jnp.pad(fields.transpose(1, 0, 2), ((0, 0), (0, CP - 69), (0, 0)))
-    wc = jnp.pad(conv_weight.reshape(64, 3, 3, 69), ((0, 0), (0, 0), (0, 0), (0, CP - 69)))
-    wc = jnp.pad(wc.reshape(64, 3, 3 * CP), ((0, 0), (0, 0), (0, 16))).transpose(1, 0, 2)
-    embedded, embed_gradient, conv_gradient = step(t, wc, embed_weight, token_grads.reshape(512, 1024))
+    embedded, embed_gradient, conv_gradient = step(t, conv_weight.transpose(1, 0, 2), embed_weight, token_grads.reshape(512, 1024))
+    specs = [
+        pl.BlockSpec((128, 512), lambda n: (n, 0)),
+        pl.BlockSpec((64, 128), lambda n: (0, 0)),
+        pl.BlockSpec((9, 64, 69), lambda n: (0, 0, 0)),
+    ]
+    embedded, embed_gradient, conv_gradient = pl.pallas_call(
+        settle,
+        grid=(4,),
+        out_shape=tuple(jax.ShapeDtypeStruct(a.shape, a.dtype) for a in (embedded, embed_gradient, conv_gradient)),
+        in_specs=specs,
+        out_specs=tuple(specs),
+    )(embedded, embed_gradient, conv_gradient)
     return embedded.reshape(1, 1, 512, 512), conv_gradient.transpose(1, 0, 2), embed_gradient
 
 

time: 95.2 us -> 77.6 us (0.82)
  the two profiles are of different devices: /device:TPU:1 before, /device:TPU:6 now
where the time goes in v2:
time: 77.6 us; the launch traced here: 77.4 us
  Pallas kernels  73.6 us (95%)
  local copies, waits for them, and re-layouts  3.16 us (4%)
    pallas_call x1, Pallas kernels, step(): pl.pallas_call(kernel, out_shape=(jax.ShapeDtypeStruct((512, 512), BF), j...  70.2 us
    pallas_call x1, Pallas kernels, body(): pl.pallas_call(settle, grid=(4,), out_shape=tuple((jax.ShapeDtypeStruct(a...  3.45 us
    unnamed x1, local copies, waits for them, and re-layouts  1.99 us

profile of v2, /device:TPU:6, one launch (start us, length us, event | category | flops | bytes accessed | tf_op | source)
XLA Modules:
  0.0 77.4 jit_solution(6941108588339151854)
XLA Ops:
  0.6 2.0 %copy.9 = bf16[69,64,128]{2,0,1:T(8,128)(2,1)S(1)} copy(bf16[69,64,128]{2,1,0:T(8,128)(2,1)} %param.4) | data formatting | bytes 2260992 | tf_op args[0]
  2.6 1.2 %pad.4.t_ref = bf16[64,80,128]{2,1,0:T(8,128)(2,1)} pad(bf16[64,69,128]{2,1,0:T(8,128)(2,1)S(1)} %bitcast.7, bf16[]{:T(256)} %constant.2.clone.1), padding=0_0x0_11x0_0 | pad | bytes 2441218 | tf_op jit(solution)/shard_map/jit(_pad)/pad | solution.py:522
  3.8 70.2 %shard_map.67 = (bf16[512,512]{1,0:T(8,128)(2,1)}, f32[64,128]{1,0:T(8,128)}, f32[9,64,69]{2,1,0:T(8,128)}) custom-call(bf16[64,80,128]{2,1,0:T(8,128)(2,1)} %pad.4.t_ref, bf16[9,64,69]{2,1,0:T(8,128)(2,1)} %bitcast.9, bf16[128,16384]{1,0:T(8,128)(2,1)} %w_ref.1, bf16[512,1024]{1,0:T(8,128)(2,1)} %bitcast.8), custom_call_target="tpu_custom_call" | custom-call | tf_op jit(solution)/shard_map/pallas_call | solution.py:498
  74.0 3.5 %shard_map.68 = (bf16[512,512]{1,0:T(8,128)(2,1)}, f32[64,128]{1,0:T(8,128)}, f32[9,64,69]{2,1,0:T(8,128)}) custom-call(bf16[512,512]{1,0:T(8,128)(2,1)} %get-tuple-element.9.emb, f32[64,128]{1,0:T(8,128)} %get-tuple-element.10.eg, f32[9,64,69]{2,1,0:T(8,128)} %get-tuple-element.11.cg), custom_call_target="tpu_custom_call" | custom-call | tf_op jit(solution)/shard_map/pallas_call | solution.py:529

commit v3 on v2

--- a/solution.py
+++ b/solution.py
@@ -27,12 +27,12 @@
 def kernel(
     t_ref, wc_ref, w_ref, tg_ref,
     emb_out, eg_out, cg_out,
-    slab, halo_l, halo_r, got_l, got_r, pack_l, pack_r,
+    narrow, wide, edge, slab, halo_l, halo_r, got_l, got_r, pack_l, pack_r,
     wc, wv, tgo, tgp, src, p1, xs, hid, hidp, hidt, dgelu, emb,
-    egb, ego, ra, sbf, sbb, rb, scf, scb, rc,
-    cga, cgp, scg, rcg, l0, rl, l1, agb, full,
+    ysb, yrb, yown, yxs, yxr, ycf, xsb, xrb, xown, xys, xyr, xcf, scf, scb, rc,
+    cga, cgp, scg, scb16, rcg, l0, rl, l1, agb, full,
     loc, tg_s, tg_r, ha_s, ha_r, pk_s, pk_r, wc_s, wc_r, em_s, em_r, tf_s, tf_r, hp_s, hp_r,
-    a_s, a_r, b_s, b_r, c_s, c_r, q_s, q_r, d_s, d_r, e_s, e_r, f_s, f_r,
+    ya_s, ya_r, yb_s, yb_r, xa_s, xa_r, xb_s, xb_r, c_s, c_r, q_s, q_r, d_s, d_r, e_s, e_r, f_s, f_r,
 ):
     lon = lax.axis_index("lon")
     lat = lax.axis_index("lat")
@@ -71,8 +71,8 @@
         greet(lax.rem(lon + 1, 16), lat + 1, ch)
         greet(lax.rem(lon + 15, 16), lat + 1, ch)
 
-    slab_copy = pltpu.make_async_copy(t_ref.at[pl.ds(31 * ch, 33)], slab.at[pl.ds(other, 33)], loc.at[0])
-    slab_copy.start()
+    field_copy = pltpu.make_async_copy(t_ref, narrow, loc.at[0])
+    field_copy.start()
 
     own_half = pl.ds(pl.multiple_of(64 * ch, 64), 64)
     for da in range(3):
@@ -94,12 +94,21 @@
     xs[:, 480:496, :] = jnp.zeros((6, 16, 256), BF)
     cga[...] = jnp.zeros_like(cga)
 
-    slab_copy.wait()
+    wide[4416:5120] = jnp.zeros((704, 128), F32)
+    field_copy.wait()
+
+    def widen(c, _):
+        wide[pl.ds(pl.multiple_of(64 * c, 64), 64)] = narrow[c].astype(F32)
+        return 0
+
+    lax.fori_loop(0, 69, widen, 0, unroll=3)
+    edge[...] = wide[pl.ds(63 * other, CP, stride=64)].astype(BF)
     lane = lax.broadcasted_iota(jnp.int32, (CP, 128), 1)
     left = jnp.zeros((CP, 128), F32)
     right = jnp.zeros((CP, 128), F32)
     for m in range(33):
-        row = slab[other + m].astype(F32)
+        row = wide[pl.ds(31 * ch + m, CP, stride=64)]
+        slab[other + m] = row.astype(BF)
         if m:
             row = pltpu.roll(row, m, 1)
         left = jnp.where(lane == (m + 127) % 128, row, left)
@@ -114,18 +123,18 @@
     def _():
         pl.semaphore_wait(barrier, 42)
 
-    def halo_copies(row, to_lat, base):
+    def halo_copies(to_lat, base):
         out = []
         for n, (shift, target) in enumerate(((0, slab.at[33 * ch]), (1, halo_l), (15, halo_r))):
             to = lax.rem(base + shift, 16)
-            out.append(remote(t_ref.at[row], target, ha_s.at[n], ha_r.at[n], to, to_lat, ch))
+            out.append(remote(edge, target, ha_s.at[n], ha_r.at[n], to, to_lat, ch))
         return out
 
-    inner = halo_copies(63 * other, lat + 1 - 2 * ch, lon)
+    inner = halo_copies(lat + 1 - 2 * ch, lon)
     polar_s = []
     for n, (shift, target) in enumerate(((0, slab.at[33 * ch]), (1, halo_l), (15, halo_r))):
         to = lax.rem(lon + 8 + shift, 16)
-        polar_s.append(remote(t_ref.at[63 * ch], target, ha_s.at[3 + n], ha_r.at[n], to, lat, ch))
+        polar_s.append(remote(slab.at[1 + 31 * ch], target, ha_s.at[3 + n], ha_r.at[n], to, lat, ch))
     has_inner = lat != 7 * other
     has_polar = lat == 7 * ch
 
@@ -225,10 +234,9 @@
         hidt[:, pl.ds(pl.multiple_of(128 * s, 128), 128)] = h.T
         return 0
 
-    lax.fori_loop(0, 16, conv, 0)
+    lax.fori_loop(0, 16, conv, 0, unroll=2)
     hp = remote(hid.at[:, other], hidp, hp_s, hp_r, lon, lat, other)
     hp.start()
-
     for c in w_copies:
         c.wait()
 
@@ -267,156 +275,197 @@
                 def _(g=g):
                     emb_copies[0, g].start()
 
-    def a_copy(cc, n):
-        rows = pl.ds(pl.multiple_of(256 * cc, 256), 256)
+    def ya_copy(n):
         return remote(
-            egb.at[n - 1, rows], ra.at[n - 1, rows], a_s.at[cc, n - 1], a_r.at[cc, n - 1],
-            lon, lax.rem(lat + 2 * n, 8), ch,
+            ysb.at[n - 1], yrb.at[n - 1], ya_s.at[n - 1], ya_r.at[n - 1], lon, lax.rem(lat + 2 * n, 8), ch
         )
 
-    def eg_part(cc, n):
-        columns = pl.ds(pl.multiple_of(256 * lax.rem(y + n, 4), 256), 256)
-        mine = hid[pl.ds(4 * cc, 4), ch].reshape(256, 256)
-        theirs = hidp[pl.ds(4 * cc, 4)].reshape(256, 256)
-        return dot(mine, tgo[:, columns]) + dot(theirs, tgp[:, columns])
-
-    forwards = []
+    def yb_copy():
+        return remote(yxs, yxr, yb_s, yb_r, lon, lat + 1 - 2 * xlo, ch)
+
+    def xa_copy(n):
+        return remote(xsb.at[n], xrb.at[n], xa_s.at[n], xa_r.at[n], lon, lat + 1 - 2 * xlo, ch)
+
+    def xb_copy(n):
+        return remote(
+            xys.at[n - 1], xyr.at[n - 1], xb_s.at[n - 1], xb_r.at[n - 1], lon, lax.rem(lat + 2 * n, 8), ch
+        )
+
+    def split(value):
+        first, second = value[:, 0:128], value[:, 128:256]
+        return jnp.where(xlo == 0, first, second), jnp.where(xlo == 0, second, first)
+
+    def block(n):
+        return pl.ds(pl.multiple_of(256 * lax.rem(y + n, 4), 256), 256)
+
+    def embed_part(n):
+        def some(c, _):
+            mine = hid[pl.ds(4 * c, 4), ch].reshape(256, 256)
+            theirs = hidp[pl.ds(4 * c, 4)].reshape(256, 256)
+            part = dot(mine, tgo[:, block(n)]) + dot(theirs, tgp[:, block(n)])
+
+            @pl.when(c < 2)
+            def _():
+                rows = pl.ds(pl.multiple_of(256 * c, 256), 256)
+                if n:
+                    ysb[n - 1, rows] = part.astype(BF)
+                else:
+                    yown[rows] = part
+
+            @pl.when(c >= 2)
+            def _():
+                rows = pl.ds(pl.multiple_of(256 * (c - 2), 256), 256)
+                near, far = split(part)
+                xown[n, rows] = near
+                xsb[n, rows] = far.astype(BF)
+
+            return 0
+
+        lax.fori_loop(0, 4, some, 0)
+        xa_copy(n).start()
+        if n:
+            ya_copy(n).start()
+
+    def stage_xb(n):
+        xa_copy(n).wait_recv()
+        total = xown[n] + xrb[n].astype(F32)
+        if n:
+            xys[n - 1] = total.astype(BF)
+            xb_copy(n).start()
+        else:
+            xcf[...] = total
+
+    forwards = {}
+    last = None
     for n in order:
         for i in range(8):
             tg_copies[n, i].wait_recv()
-        columns = pl.ds(pl.multiple_of(256 * lax.rem(y + n, 4), 256), 256)
-        c = remote(tgo.at[:, columns], tgp.at[:, columns], tf_s.at[n], tf_r.at[n], lon, lat, other)
-        c.start()
-        forwards.append(c)
-        if n == 2:
+        forwards[n] = remote(tgo.at[:, block(n)], tgp.at[:, block(n)], tf_s.at[n], tf_r.at[n], lon, lat, other)
+        forwards[n].start()
+        if last is None:
             hp.wait_recv()
-        c.wait_recv()
-
-        def stage_a(cc, _, n=n):
-            rows = pl.ds(pl.multiple_of(256 * cc, 256), 256)
-            if n:
-                egb[n - 1, rows] = eg_part(cc, n).astype(BF)
-                a_copy(cc, n).start()
-            else:
-                ego[rows] = eg_part(cc, 0)
-            return 0
-
-        lax.fori_loop(0, 4, stage_a, 0)
-
+        else:
+            forwards[last].wait_recv()
+            embed_part(last)
+        last = n
 
     def conv_grad(a, _):
         hg = dot(wv[pl.ds(4 * a, 4)].reshape(512, 1024), tgo[...], NT)
         pg = (hg * dgelu[pl.ds(4 * a, 4)].reshape(512, 256)).astype(BF)
-        for b in range(4):
-            for da in range(3):
-                cga[da] += dot(pg[128 * b : 128 * b + 128], xs[a + da, CP * b : CP * b + 256, :], NT)
+        for da in range(3):
+            total = cga[da]
+            for b in range(4):
+                total = total + dot(pg[128 * b : 128 * b + 128], xs[a + da, CP * b : CP * b + 256, :], NT)
+            cga[da] = total
         return 0
 
-    lax.fori_loop(0, 4, conv_grad, 0)
-    theirs = pl.ds(pl.multiple_of(64 * other, 64), 64)
-    q_copy = remote(cga.at[:, theirs, :], cgp, q_s, q_r, lon, lat, other)
+    lax.fori_loop(0, 4, conv_grad, 0, unroll=2)
+    half_o = pl.ds(pl.multiple_of(64 * other, 64), 64)
+    q_copy = remote(cga.at[:, half_o, :], cgp, q_s, q_r, lon, lat, other)
     q_copy.start()
-
-    def b_copy(cc):
-        rows = pl.ds(pl.multiple_of(256 * cc, 256), 256)
-        return remote(sbb.at[other_x, rows], rb.at[rows], b_s.at[cc], b_r.at[cc], lon, lat + 1 - 2 * xlo, ch)
-
-    other_x = 1 - xlo
-
-    def stage_b(cc, _):
-        rows = pl.ds(pl.multiple_of(256 * cc, 256), 256)
-        total = ego[rows]
-        for n in (1, 3, 2):
-            a_copy(cc, n).wait_recv()
-            total = total + ra[n - 1, rows].astype(F32)
-        for g in range(2):
-            piece = total[:, 128 * g : 128 * g + 128]
-            sbf[g, rows] = piece
-            sbb[g, rows] = piece.astype(BF)
-        b_copy(cc).start()
-        return 0
+    forwards[0].wait_recv()
+    embed_part(0)
+    stage_xb(2)
+    stage_xb(1)
+
+    def d_copy(j):
+        i = lax.rem(j - lon + 16, 16)
+        return remote(scb16.at[j], rcg.at[i], d_s.at[j], d_r.at[i], j, lat, ch)
+
+    def e_copy(i):
+        return remote(l0, rl.at[lat], e_s.at[i], e_r.at[i], lon, lax.rem(lat + i, 8), ch)
+
+    def f_copy(i):
+        return remote(l1, agb.at[lon], f_s.at[i], f_r.at[lon], lax.rem(lon + i, 16), lat, ch)
+
+    q_copy.wait_recv()
+    total = cga[:, pl.ds(pl.multiple_of(64 * ch, 64), 64), :] + cgp[...]
+    for j in range(12):
+        for half in range(2):
+            piece = total[j // 4, 16 * (j % 4) : 16 * (j % 4) + 16, 128 * half : 128 * half + 128]
+            scg[j, half] = piece
+            scb16[j, half] = piece.astype(BF)
+    for j in range(12):
+
+        @pl.when(j != lon)
+        def _(j=j):
+            d_copy(j).start()
+
+    stage_xb(3)
+    stage_xb(0)
+
+    total = yown[...]
+    for n in (1, 3, 2):
+        ya_copy(n).wait_recv()
+        total = total + yrb[n - 1].astype(F32)
+    near, far = split(total)
+    ycf[...] = near
+    yxs[...] = far.astype(BF)
+    yb_copy().start()
+
+    @pl.when(lon < 12)
+    def _():
+        total = scg[lon]
+        for i in range(1, 16):
+            remote(scb16.at[0], rcg.at[i], d_s.at[0], d_r.at[i], lon, lat, other).wait_recv()
+            total = total + rcg[i].astype(F32)
+        l0[...] = total
+        rl[lat] = total
+        for i in range(1, 8):
+            e_copy(i).start()
 
     def c_copy(s):
         i = lax.rem(s - lon + 16, 16)
         return remote(scb.at[s], rc.at[i], c_s.at[i], c_r.at[i], s, lat, ch)
 
-    def stage_c(cc, _):
-        rows = pl.ds(pl.multiple_of(256 * cc, 256), 256)
-        b_copy(cc).wait_recv()
-        total = (sbf[xlo, rows] + rb[rows].astype(F32)).reshape(4, 64, 128)
-        scf[pl.ds(4 * cc, 4)] = total
-        scb[pl.ds(4 * cc, 4)] = total.astype(BF)
-        for k in range(4):
-            s = 4 * cc + k
+    def stage_c(first, total):
+        total = total.reshape(8, 64, 128)
+        scf[first : first + 8] = total
+        scb[first : first + 8] = total.astype(BF)
+        for s in range(first, first + 8):
 
             @pl.when(s != lon)
-            def _():
+            def _(s=s):
                 c_copy(s).start()
 
-        return 0
-
-    def d_copy(i):
-        to = lax.rem(lon + i, 16)
-        return remote(scg.at[to], rcg.at[i], d_s.at[i], d_r.at[i], to, lat, ch)
-
-    def e_copy(i):
-        return remote(l0, rl.at[lat], e_s.at[i], e_r.at[i], lon, lax.rem(lat + i, 8), ch)
-
-    def f_copy(i):
-        return remote(l1, agb.at[lon], f_s.at[i], f_r.at[i], lax.rem(lon + i, 16), lat, ch)
-
-    q_copy.wait_recv()
-    total = cga[:, pl.ds(pl.multiple_of(64 * ch, 64), 64), :] + cgp[...]
-    for n in range(16):
-        ob, half = n // 2, n % 2
-        scg[n] = total[:, 8 * ob : 8 * ob + 8, 128 * half : 128 * half + 128]
-    for i in range(1, 16):
-        d_copy(i).start()
-
-    stage_b(0, 0)
-
-    total = scg[lon]
-    for i in range(1, 16):
-        d_copy(i).wait_recv()
-        total = total + rcg[i]
-    l0[...] = total
-    rl[lat] = total
-    for i in range(1, 8):
-        e_copy(i).start()
-
-    stage_b(1, 0)
-    stage_c(0, 0)
-
-    for i in range(1, 8):
-        e_copy(i).wait_recv()
-    total = rl[0]
-    for i in range(1, 8):
-        total = total + rl[i]
-    l1[...] = total
-    agb[lon] = total
-    for i in range(1, 16):
-        f_copy(i).start()
-
-    stage_b(2, 0)
-    stage_c(1, 0)
-    stage_b(3, 0)
-    stage_c(2, 0)
-
-    for i in range(1, 16):
-        f_copy(i).wait_recv()
-    for n in range(16):
-        ob, half = n // 2, n % 2
-        full[:, 8 * ob : 8 * ob + 8, 128 * half : 128 * half + 128] = agb[n]
-    for da in range(3):
-        for db in range(3):
-            cg_out[3 * da + db] = full[da, :, CP * db : CP * db + 69]
-
-    stage_c(3, 0)
+    total = xcf[...]
+    for n in (1, 3, 2):
+        xb_copy(n).wait_recv()
+        total = total + xyr[n - 1].astype(F32)
+    stage_c(8, total)
+    yb_copy().wait_recv()
+    stage_c(0, ycf[...] + yxr[...].astype(F32))
+
+    @pl.when(lon < 12)
+    def _():
+        for i in range(1, 8):
+            e_copy(i).wait_recv()
+        total = rl[0]
+        for i in range(1, 8):
+            total = total + rl[i]
+        total = total.astype(BF)
+        l1[...] = total
+        agb[lon] = total
+        for i in range(1, 16):
+            f_copy(i).start()
+
     total = scf[lon]
     for i in range(1, 16):
         remote(scb.at[0], rc.at[i], c_s.at[i], c_r.at[i], lon, lat, other).wait_recv()
         total = total + rc[i].astype(F32)
     eg_out[...] = total
+
+    for j in range(12):
+
+        @pl.when(j != lon)
+        def _(j=j):
+            remote(l1, agb.at[j], f_s.at[0], f_r.at[j], lon, lat, other).wait_recv()
+
+        for half in range(2):
+            full[j // 4, 16 * (j % 4) : 16 * (j % 4) + 16, 128 * half : 128 * half + 128] = agb[j, half].astype(F32)
+    for da in range(3):
+        for db in range(3):
+            cg_out[3 * da + db] = full[da, :, CP * db : CP * db + 69]
 
     for i in range(8):
         for g in range(2):
@@ -449,7 +498,7 @@
     pk1.wait_send()
     hp.wait_send()
     q_copy.wait_send()
-    for c in forwards:
+    for c in forwards.values():
         c.wait_send()
     for (i, g), c in emb_copies.items():
         if i:
@@ -460,38 +509,50 @@
             def _(c=c):
                 c.wait_send()
 
-    for cc in range(4):
-        for n in (1, 2, 3):
-            a_copy(cc, n).wait_send()
-        b_copy(cc).wait_send()
+    for n in (1, 2, 3):
+        ya_copy(n).wait_send()
+        xb_copy(n).wait_send()
+    yb_copy().wait_send()
+    for n in range(4):
+        xa_copy(n).wait_send()
     for i in range(1, 16):
         remote(scb.at[0], rc.at[i], c_s.at[i], c_r.at[i], lon, lat, other).wait_send()
-        d_copy(i).wait_send()
-        f_copy(i).wait_send()
-    for i in range(1, 8):
-        e_copy(i).wait_send()
+    for j in range(12):
+
+        @pl.when(j != lon)
+        def _(j=j):
+            d_copy(j).wait_send()
+
+    @pl.when(lon < 12)
+    def _():
+        for i in range(1, 16):
+            f_copy(i).wait_send()
+        for i in range(1, 8):
+            e_copy(i).wait_send()
 
 
 def step(t, wc, w, tg):
     vm = pltpu.VMEM
     sem = pltpu.SemaphoreType.DMA
     scratch = [
-        vm((34, CP, 128), BF), vm((CP, 128), BF), vm((CP, 128), BF), vm((CP, 128), BF), vm((CP, 128), BF),
+        vm((69, 64, 128), BF), vm((64 * CP, 128), F32), vm((CP, 128), BF), vm((34, CP, 128), BF), vm((CP, 128), BF), vm((CP, 128), BF), vm((CP, 128), BF), vm((CP, 128), BF),
         vm((CP, 128), BF), vm((CP, 128), BF),
         vm((3, 128, 256), BF), vm((16, 128, 1024), BF), vm((256, 1024), BF), vm((256, 1024), BF),
         vm((6, 2 * CP, 512), BF), vm((512, 768), BF), vm((6, 496, 256), BF),
         vm((16, 2, 64, 256), BF), vm((16, 64, 256), BF), vm((256, 2048), BF), vm((16, 128, 256), F32),
         vm((2, 256, 512), BF),
-        vm((3, 1024, 256), BF), vm((1024, 256), F32), vm((3, 1024, 256), BF),
-        vm((2, 1024, 128), F32), vm((2, 1024, 128), BF), vm((1024, 128), BF),
+        vm((3, 512, 256), BF), vm((3, 512, 256), BF), vm((512, 256), F32),
+        vm((512, 128), BF), vm((512, 128), BF), vm((512, 128), F32),
+        vm((4, 512, 128), BF), vm((4, 512, 128), BF), vm((4, 512, 128), F32),
+        vm((3, 512, 128), BF), vm((3, 512, 128), BF), vm((512, 128), F32),
         vm((16, 64, 128), F32), vm((16, 64, 128), BF), vm((16, 64, 128), BF),
-        vm((3, 128, 256), F32), vm((3, 64, 256), F32), vm((16, 3, 8, 128), F32), vm((16, 3, 8, 128), F32),
-        vm((3, 8, 128), F32), vm((8, 3, 8, 128), F32), vm((3, 8, 128), F32), vm((16, 3, 8, 128), F32),
-        vm((3, 64, 256), F32),
+        vm((3, 128, 256), F32), vm((3, 64, 256), F32), vm((12, 2, 16, 128), F32), vm((12, 2, 16, 128), BF),
+        vm((16, 2, 16, 128), BF), vm((2, 16, 128), F32), vm((8, 2, 16, 128), F32), vm((2, 16, 128), BF),
+        vm((12, 2, 16, 128), BF), vm((3, 64, 256), F32),
         sem((18,)), sem((4, 8)), sem((4, 8)), sem((6,)), sem((3,)), sem((2,)), sem((2,)), sem, sem,
         sem((16,)), sem((16,)), sem((4,)), sem((4,)), sem, sem,
-        sem((4, 3)), sem((4, 3)), sem((4,)), sem((4,)), sem((16,)), sem((16,)), sem, sem,
-        sem((16,)), sem((16,)), sem((8,)), sem((8,)), sem((16,)), sem((16,)),
+        sem((3,)), sem((3,)), sem, sem, sem((4,)), sem((4,)), sem((3,)), sem((3,)), sem((16,)), sem((16,)), sem, sem,
+        sem((12,)), sem((16,)), sem((8,)), sem((8,)), sem((16,)), sem((12,)),
     ]
     any_ = pl.BlockSpec(memory_space=pl.ANY)
     inside = pl.BlockSpec(memory_space=pltpu.VMEM)
@@ -509,29 +570,35 @@
     )(t, wc, w, tg)
 
 
-def settle(emb, eg, cg, emb_out, eg_out, cg_out):
-    emb_out[...] = emb[...]
-
-    @pl.when(pl.program_id(0) == 0)
-    def _():
-        eg_out[...] = eg[...]
-        cg_out[...] = cg[...]
+def settle(emb, eg, cg, emb_out, eg_out, cg_out, emb_held, eg_held, cg_held, sem):
+    moves = []
+    for n in range(4):
+        rows = pl.ds(128 * n, 128)
+        moves.append((emb.at[rows], emb_held.at[rows], emb_out.at[rows]))
+    moves += [(eg, eg_held, eg_out), (cg, cg_held, cg_out)]
+    moves = [
+        (pltpu.make_async_copy(a, b, sem.at[0, n]), pltpu.make_async_copy(b, c, sem.at[1, n]))
+        for n, (a, b, c) in enumerate(moves)
+    ]
+    for first, _ in moves:
+        first.start()
+    for first, second in moves:
+        first.wait()
+        second.start()
+    for _, second in moves:
+        second.wait()
 
 
 def body(fields, conv_weight, embed_weight, token_grads):
-    t = jnp.pad(fields.transpose(1, 0, 2), ((0, 0), (0, CP - 69), (0, 0)))
-    embedded, embed_gradient, conv_gradient = step(t, conv_weight.transpose(1, 0, 2), embed_weight, token_grads.reshape(512, 1024))
-    specs = [
-        pl.BlockSpec((128, 512), lambda n: (n, 0)),
-        pl.BlockSpec((64, 128), lambda n: (0, 0)),
-        pl.BlockSpec((9, 64, 69), lambda n: (0, 0, 0)),
-    ]
+    embedded, embed_gradient, conv_gradient = step(fields, conv_weight.transpose(1, 0, 2), embed_weight, token_grads.reshape(512, 1024))
+    shapes = [(a.shape, a.dtype) for a in (embedded, embed_gradient, conv_gradient)]
+    outside = pl.BlockSpec(memory_space=pltpu.HBM)
     embedded, embed_gradient, conv_gradient = pl.pallas_call(
         settle,
-        grid=(4,),
-        out_shape=tuple(jax.ShapeDtypeStruct(a.shape, a.dtype) for a in (embedded, embed_gradient, conv_gradient)),
-        in_specs=specs,
-        out_specs=tuple(specs),
+        out_shape=tuple(jax.ShapeDtypeStruct(*a) for a in shapes),
+        in_specs=[outside] * 3,
+        out_specs=(outside,) * 3,
+        scratch_shapes=[pltpu.VMEM(*a) for a in shapes] + [pltpu.SemaphoreType.DMA((2, 6))],
     )(embedded, embed_gradient, conv_gradient)
     return embedded.reshape(1, 1, 512, 512), conv_gradient.transpose(1, 0, 2), embed_gradient
 

time: 77.6 us -> 69.2 us (0.89)
  the two profiles are of different devices: /device:TPU:6 before, /device:TPU:1 now
where the time goes in v3:
time: 69.2 us; the launch traced here: 69.1 us
  Pallas kernels  68.5 us (99%)
    pallas_call x1, Pallas kernels, step(): pl.pallas_call(kernel, out_shape=(jax.ShapeDtypeStruct((512, 512), BF), j...  66.4 us
    pallas_call x1, Pallas kernels, body(): pl.pallas_call(settle, out_shape=tuple((jax.ShapeDtypeStruct(*a) for a in...  2.06 us

profile of v3, /device:TPU:1, one launch (start us, length us, event | category | flops | bytes accessed | tf_op | source)
XLA Modules:
  0.0 69.1 jit_solution(3428037674553238440)
XLA Ops:
  0.6 66.4 %shard_map.67 = (bf16[512,512]{1,0:T(8,128)(2,1)}, f32[64,128]{1,0:T(8,128)}, f32[9,64,69]{2,1,0:T(8,128)}) custom-call(bf16[69,64,128]{2,1,0:T(8,128)(2,1)} %t_ref.1, bf16[9,64,69]{2,1,0:T(8,128)(2,1)} %bitcast.5, bf16[128,16384]{1,0:T(8,128)(2,1)} %w_ref.1, bf16[512,1024]{1,0:T(8,128)(2,1)} %bitcast.4), custom_call_target="tpu_custom_call" | custom-call | tf_op jit(solution)/shard_map/pallas_call | solution.py:559
  67.1 2.1 %shard_map.68 = (bf16[512,512]{1,0:T(8,128)(2,1)}, f32[64,128]{1,0:T(8,128)}, f32[9,64,69]{2,1,0:T(8,128)}) custom-call(bf16[512,512]{1,0:T(8,128)(2,1)} %get-tuple-element.9.emb, f32[64,128]{1,0:T(8,128)} %get-tuple-element.10.eg, f32[9,64,69]{2,1,0:T(8,128)} %get-tuple-element.11.cg), custom_call_target="tpu_custom_call" | custom-call | tf_op jit(solution)/shard_map/pallas_call | solution.py:596

commit v4 on v3

--- a/solution.py
+++ b/solution.py
@@ -32,7 +32,7 @@
     ysb, yrb, yown, yxs, yxr, ycf, xsb, xrb, xown, xys, xyr, xcf, scf, scb, rc,
     cga, cgp, scg, scb16, rcg, l0, rl, l1, agb, full,
     loc, tg_s, tg_r, ha_s, ha_r, pk_s, pk_r, wc_s, wc_r, em_s, em_r, tf_s, tf_r, hp_s, hp_r,
-    ya_s, ya_r, yb_s, yb_r, xa_s, xa_r, xb_s, xb_r, c_s, c_r, q_s, q_r, d_s, d_r, e_s, e_r, f_s, f_r,
+    a_s, a_r, b_s, b_r, xa_s, xa_r, xb_s, xb_r, c_s, c_r, q_s, q_r, d_s, d_r, e_s, e_r, f_s, f_r,
 ):
     lon = lax.axis_index("lon")
     lat = lax.axis_index("lat")
@@ -101,7 +101,7 @@
         wide[pl.ds(pl.multiple_of(64 * c, 64), 64)] = narrow[c].astype(F32)
         return 0
 
-    lax.fori_loop(0, 69, widen, 0, unroll=3)
+    lax.fori_loop(0, 69, widen, 0, unroll=23)
     edge[...] = wide[pl.ds(63 * other, CP, stride=64)].astype(BF)
     lane = lax.broadcasted_iota(jnp.int32, (CP, 128), 1)
     left = jnp.zeros((CP, 128), F32)
@@ -156,29 +156,23 @@
     wc_remote = remote(wc.at[:, own_half], wc.at[:, own_half], wc_s, wc_r, lon, lat, other)
     wc_remote.start()
 
-    order = (2, 1, 3, 0)
-    tg_copies = {}
-    for n in order:
-        columns = pl.ds(pl.multiple_of(256 * lax.rem(y + n, 4), 256), 256)
-        for i in (4, 3, 5, 2, 6, 1, 7, 0):
-            to = 8 * ch + lax.rem(lo + i, 8)
-            rows = pl.ds(pl.multiple_of(32 * to, 32), 32)
-            place = pl.ds(pl.multiple_of(32 * lo, 32), 32)
-            c = remote(
-                tg_ref.at[rows, columns], tgo.at[place, columns], tg_s.at[n, i], tg_r.at[n, i], to, lat, hi,
-            )
-            tg_copies[n, i] = c
-            if i:
-                c.start()
-            else:
-
-                @pl.when(ch == hi)
-                def _():
-                    pltpu.make_async_copy(tg_ref.at[rows, columns], tgo.at[place, columns], tg_r.at[n, 0]).start()
-
-                @pl.when(ch != hi)
-                def _():
-                    c.start()
+    tg_copies = []
+    for i in range(8):
+        to = 8 * ch + lax.rem(lo + i, 8)
+        rows = pl.ds(pl.multiple_of(32 * to, 32), 32)
+        place = pl.ds(pl.multiple_of(32 * lo, 32), 32)
+        tg_copies.append(remote(tg_ref.at[rows], tgo.at[place], tg_s.at[i], tg_r.at[i], to, lat, hi))
+    tg_own = pltpu.make_async_copy(tg_ref.at[pl.ds(pl.multiple_of(32 * lon, 32), 32)], tgo.at[place], tg_r.at[0])
+    for i in (4, 3, 5, 2, 6, 1, 7):
+        tg_copies[i].start()
+
+    @pl.when(ch == hi)
+    def _():
+        tg_own.start()
+
+    @pl.when(ch != hi)
+    def _():
+        tg_copies[0].start()
 
     for c in inner:
         c.wait_recv()
@@ -189,7 +183,7 @@
                 src[u, pl.ds(CP * half, CP), 128 * k : 128 * k + 128] = slab[16 * half + 4 * k + u]
         return 0
 
-    lax.fori_loop(0, 6, gather_rows, 0)
+    lax.fori_loop(0, 6, gather_rows, 0, unroll=2)
     pk0.wait_recv()
     pk1.wait_recv()
     edges = jnp.concatenate([got_l[...], got_r[...], halo_l[...], halo_r[...]], axis=1)
@@ -213,7 +207,7 @@
             xs[u, CP * 5 : CP * 6, lanes] = (part[:, 640:768] + fill[:, 128:256]).astype(BF)
         return 0
 
-    lax.fori_loop(0, 6, depth, 0)
+    lax.fori_loop(0, 6, depth, 0, unroll=2)
 
     wc_remote.wait_recv()
 
@@ -234,7 +228,7 @@
         hidt[:, pl.ds(pl.multiple_of(128 * s, 128), 128)] = h.T
         return 0
 
-    lax.fori_loop(0, 16, conv, 0, unroll=2)
+    lax.fori_loop(0, 16, conv, 0, unroll=4)
     hp = remote(hid.at[:, other], hidp, hp_s, hp_r, lon, lat, other)
     hp.start()
     for c in w_copies:
@@ -248,7 +242,7 @@
         emb[n // 2, :, pl.ds(pl.multiple_of(256 * (n % 2), 256), 256)] = part.astype(BF)
         return 0
 
-    lax.fori_loop(0, 4, embed, 0)
+    lax.fori_loop(0, 4, embed, 0, unroll=2)
     emb_copies = {}
     for i in (4, 3, 5, 2, 6, 1, 7, 0):
         r = lax.rem(lo + i, 8)
@@ -275,79 +269,94 @@
                 def _(g=g):
                     emb_copies[0, g].start()
 
-    def ya_copy(n):
+    def ya_copy(cc, n):
         return remote(
-            ysb.at[n - 1], yrb.at[n - 1], ya_s.at[n - 1], ya_r.at[n - 1], lon, lax.rem(lat + 2 * n, 8), ch
+            ysb.at[cc, n - 1], yrb.at[cc, n - 1], a_s.at[cc, n - 1], a_r.at[cc, n - 1],
+            lon, lax.rem(lat + 2 * n, 8), ch,
         )
 
-    def yb_copy():
-        return remote(yxs, yxr, yb_s, yb_r, lon, lat + 1 - 2 * xlo, ch)
-
-    def xa_copy(n):
-        return remote(xsb.at[n], xrb.at[n], xa_s.at[n], xa_r.at[n], lon, lat + 1 - 2 * xlo, ch)
-
-    def xb_copy(n):
+    def yb_copy(cc):
+        return remote(yxs.at[cc], yxr.at[cc], b_s.at[cc], b_r.at[cc], lon, lat + 1 - 2 * xlo, ch)
+
+    def xa_copy(cc):
+        return remote(xsb.at[cc], xrb.at[cc], xa_s.at[cc], xa_r.at[cc], lon, lat + 1 - 2 * xlo, ch)
+
+    def xb_copy(cc, n):
         return remote(
-            xys.at[n - 1], xyr.at[n - 1], xb_s.at[n - 1], xb_r.at[n - 1], lon, lax.rem(lat + 2 * n, 8), ch
+            xys.at[cc, n - 1], xyr.at[cc, n - 1], xb_s.at[cc, n - 1], xb_r.at[cc, n - 1],
+            lon, lax.rem(lat + 2 * n, 8), ch,
         )
 
     def split(value):
         first, second = value[:, 0:128], value[:, 128:256]
         return jnp.where(xlo == 0, first, second), jnp.where(xlo == 0, second, first)
 
-    def block(n):
-        return pl.ds(pl.multiple_of(256 * lax.rem(y + n, 4), 256), 256)
-
-    def embed_part(n):
-        def some(c, _):
-            mine = hid[pl.ds(4 * c, 4), ch].reshape(256, 256)
-            theirs = hidp[pl.ds(4 * c, 4)].reshape(256, 256)
-            part = dot(mine, tgo[:, block(n)]) + dot(theirs, tgp[:, block(n)])
-
-            @pl.when(c < 2)
-            def _():
-                rows = pl.ds(pl.multiple_of(256 * c, 256), 256)
-                if n:
-                    ysb[n - 1, rows] = part.astype(BF)
-                else:
-                    yown[rows] = part
-
-            @pl.when(c >= 2)
-            def _():
-                rows = pl.ds(pl.multiple_of(256 * (c - 2), 256), 256)
-                near, far = split(part)
-                xown[n, rows] = near
-                xsb[n, rows] = far.astype(BF)
-
-            return 0
-
-        lax.fori_loop(0, 4, some, 0)
-        xa_copy(n).start()
-        if n:
-            ya_copy(n).start()
-
-    def stage_xb(n):
-        xa_copy(n).wait_recv()
-        total = xown[n] + xrb[n].astype(F32)
-        if n:
-            xys[n - 1] = total.astype(BF)
-            xb_copy(n).start()
+    def eg_part(chunk, n):
+        columns = pl.ds(pl.multiple_of(256 * lax.rem(y + n, 4), 256), 256)
+        mine = hid[4 * chunk : 4 * chunk + 4, ch].reshape(256, 256)
+        theirs = hidp[4 * chunk : 4 * chunk + 4].reshape(256, 256)
+        return dot(mine, tgo[:, columns]) + dot(theirs, tgp[:, columns])
+
+    def stage_yb(cc):
+        total = yown[cc]
+        for n in (1, 3, 2):
+            ya_copy(cc, n).wait_recv()
+            total = total + yrb[cc, n - 1].astype(F32)
+        mine, theirs = split(total)
+        ycf[cc] = mine
+        yxs[cc] = theirs.astype(BF)
+        yb_copy(cc).start()
+
+    def stage_xb(cc):
+        xa_copy(cc).wait_recv()
+        xcf[cc] = xown[cc, :, 0:128] + xrb[cc, :, 0:128].astype(F32)
+        for n in (2, 1, 3):
+            lanes = slice(128 * n, 128 * n + 128)
+            xys[cc, n - 1] = (xown[cc, :, lanes] + xrb[cc, :, lanes].astype(F32)).astype(BF)
+            xb_copy(cc, n).start()
+
+    def c_copy(s):
+        i = lax.rem(s - lon + 16, 16)
+        return remote(scb.at[s], rc.at[i], c_s.at[i], c_r.at[i], s, lat, ch)
+
+    def stage_c(chunk):
+        if chunk < 2:
+            yb_copy(chunk).wait_recv()
+            total = ycf[chunk] + yxr[chunk].astype(F32)
         else:
-            xcf[...] = total
-
-    forwards = {}
-    last = None
-    for n in order:
-        for i in range(8):
-            tg_copies[n, i].wait_recv()
-        forwards[n] = remote(tgo.at[:, block(n)], tgp.at[:, block(n)], tf_s.at[n], tf_r.at[n], lon, lat, other)
-        forwards[n].start()
-        if last is None:
-            hp.wait_recv()
-        else:
-            forwards[last].wait_recv()
-            embed_part(last)
-        last = n
+            total = xcf[chunk - 2]
+            for n in (1, 3, 2):
+                xb_copy(chunk - 2, n).wait_recv()
+                total = total + xyr[chunk - 2, n - 1].astype(F32)
+        total = total.reshape(4, 64, 128)
+        scf[4 * chunk : 4 * chunk + 4] = total
+        scb[4 * chunk : 4 * chunk + 4] = total.astype(BF)
+        for s in range(4 * chunk, 4 * chunk + 4):
+
+            @pl.when(s != lon)
+            def _(s=s):
+                c_copy(s).start()
+
+    forwards = []
+    for i in (0, 1, 7, 2, 6, 3, 5, 4):
+        tg_copies[i].wait_recv()
+        rows = pl.ds(pl.multiple_of(32 * lax.rem(lo + 8 - i, 8), 32), 32)
+        forwards.append(remote(tgo.at[rows], tgp.at[rows], tf_s.at[i], tf_r.at[lax.rem(lo + 8 - i, 8)], lon, lat, other))
+        forwards[-1].start()
+    hp.wait_recv()
+    for c in forwards:
+        c.wait_recv()
+    for cc in range(2):
+        for n in range(4):
+            mine, theirs = split(eg_part(2 + cc, n))
+            lanes = slice(128 * n, 128 * n + 128)
+            xown[cc, :, lanes] = mine
+            xsb[cc, :, lanes] = theirs.astype(BF)
+        xa_copy(cc).start()
+        for n in (2, 1, 3):
+            ysb[cc, n - 1] = eg_part(cc, n).astype(BF)
+            ya_copy(cc, n).start()
+        yown[cc] = eg_part(cc, 0)
 
     def conv_grad(a, _):
         hg = dot(wv[pl.ds(4 * a, 4)].reshape(512, 1024), tgo[...], NT)
@@ -359,14 +368,10 @@
             cga[da] = total
         return 0
 
-    lax.fori_loop(0, 4, conv_grad, 0, unroll=2)
+    lax.fori_loop(0, 4, conv_grad, 0, unroll=4)
     half_o = pl.ds(pl.multiple_of(64 * other, 64), 64)
     q_copy = remote(cga.at[:, half_o, :], cgp, q_s, q_r, lon, lat, other)
     q_copy.start()
-    forwards[0].wait_recv()
-    embed_part(0)
-    stage_xb(2)
-    stage_xb(1)
 
     def d_copy(j):
         i = lax.rem(j - lon + 16, 16)
@@ -391,17 +396,10 @@
         def _(j=j):
             d_copy(j).start()
 
-    stage_xb(3)
     stage_xb(0)
-
-    total = yown[...]
-    for n in (1, 3, 2):
-        ya_copy(n).wait_recv()
-        total = total + yrb[n - 1].astype(F32)
-    near, far = split(total)
-    ycf[...] = near
-    yxs[...] = far.astype(BF)
-    yb_copy().start()
+    stage_yb(0)
+    stage_xb(1)
+    stage_yb(1)
 
     @pl.when(lon < 12)
     def _():
@@ -414,27 +412,9 @@
         for i in range(1, 8):
             e_copy(i).start()
 
-    def c_copy(s):
-        i = lax.rem(s - lon + 16, 16)
-        return remote(scb.at[s], rc.at[i], c_s.at[i], c_r.at[i], s, lat, ch)
-
-    def stage_c(first, total):
-        total = total.reshape(8, 64, 128)
-        scf[first : first + 8] = total
-        scb[first : first + 8] = total.astype(BF)
-        for s in range(first, first + 8):
-
-            @pl.when(s != lon)
-            def _(s=s):
-                c_copy(s).start()
-
-    total = xcf[...]
-    for n in (1, 3, 2):
-        xb_copy(n).wait_recv()
-        total = total + xyr[n - 1].astype(F32)
-    stage_c(8, total)
-    yb_copy().wait_recv()
-    stage_c(0, ycf[...] + yxr[...].astype(F32))
+    stage_c(0)
+    stage_c(2)
+    stage_c(1)
 
     @pl.when(lon < 12)
     def _():
@@ -449,6 +429,7 @@
         for i in range(1, 16):
             f_copy(i).start()
 
+    stage_c(3)
     total = scf[lon]
     for i in range(1, 16):
         remote(scb.at[0], rc.at[i], c_s.at[i], c_r.at[i], lon, lat, other).wait_recv()
@@ -485,20 +466,18 @@
             c.wait_send()
 
     wc_remote.wait_send()
-    for n in order:
-        for i in range(1, 8):
-            tg_copies[n, i].wait_send()
+    for i in range(1, 8):
+        tg_copies[i].wait_send()
 
     @pl.when(ch != hi)
     def _():
-        for n in order:
-            tg_copies[n, 0].wait_send()
+        tg_copies[0].wait_send()
 
     pk0.wait_send()
     pk1.wait_send()
     hp.wait_send()
     q_copy.wait_send()
-    for c in forwards.values():
+    for c in forwards:
         c.wait_send()
     for (i, g), c in emb_copies.items():
         if i:
@@ -509,12 +488,12 @@
             def _(c=c):
                 c.wait_send()
 
-    for n in (1, 2, 3):
-        ya_copy(n).wait_send()
-        xb_copy(n).wait_send()
-    yb_copy().wait_send()
-    for n in range(4):
-        xa_copy(n).wait_send()
+    for cc in range(2):
+        for n in (1, 2, 3):
+            ya_copy(cc, n).wait_send()
+            xb_copy(cc, n).wait_send()
+        yb_copy(cc).wait_send()
+        xa_copy(cc).wait_send()
     for i in range(1, 16):
         remote(scb.at[0], rc.at[i], c_s.at[i], c_r.at[i], lon, lat, other).wait_send()
     for j in range(12):
@@ -541,17 +520,17 @@
         vm((6, 2 * CP, 512), BF), vm((512, 768), BF), vm((6, 496, 256), BF),
         vm((16, 2, 64, 256), BF), vm((16, 64, 256), BF), vm((256, 2048), BF), vm((16, 128, 256), F32),
         vm((2, 256, 512), BF),
-        vm((3, 512, 256), BF), vm((3, 512, 256), BF), vm((512, 256), F32),
-        vm((512, 128), BF), vm((512, 128), BF), vm((512, 128), F32),
-        vm((4, 512, 128), BF), vm((4, 512, 128), BF), vm((4, 512, 128), F32),
-        vm((3, 512, 128), BF), vm((3, 512, 128), BF), vm((512, 128), F32),
+        vm((2, 3, 256, 256), BF), vm((2, 3, 256, 256), BF), vm((2, 256, 256), F32),
+        vm((2, 256, 128), BF), vm((2, 256, 128), BF), vm((2, 256, 128), F32),
+        vm((2, 256, 512), BF), vm((2, 256, 512), BF), vm((2, 256, 512), F32),
+        vm((2, 3, 256, 128), BF), vm((2, 3, 256, 128), BF), vm((2, 256, 128), F32),
         vm((16, 64, 128), F32), vm((16, 64, 128), BF), vm((16, 64, 128), BF),
         vm((3, 128, 256), F32), vm((3, 64, 256), F32), vm((12, 2, 16, 128), F32), vm((12, 2, 16, 128), BF),
         vm((16, 2, 16, 128), BF), vm((2, 16, 128), F32), vm((8, 2, 16, 128), F32), vm((2, 16, 128), BF),
         vm((12, 2, 16, 128), BF), vm((3, 64, 256), F32),
-        sem((18,)), sem((4, 8)), sem((4, 8)), sem((6,)), sem((3,)), sem((2,)), sem((2,)), sem, sem,
-        sem((16,)), sem((16,)), sem((4,)), sem((4,)), sem, sem,
-        sem((3,)), sem((3,)), sem, sem, sem((4,)), sem((4,)), sem((3,)), sem((3,)), sem((16,)), sem((16,)), sem, sem,
+        sem((18,)), sem((8,)), sem((8,)), sem((6,)), sem((3,)), sem((2,)), sem((2,)), sem, sem,
+        sem((16,)), sem((16,)), sem((8,)), sem((8,)), sem, sem,
+        sem((2, 3)), sem((2, 3)), sem((2,)), sem((2,)), sem((2,)), sem((2,)), sem((2, 3)), sem((2, 3)), sem((16,)), sem((16,)), sem, sem,
         sem((12,)), sem((16,)), sem((8,)), sem((8,)), sem((16,)), sem((12,)),
     ]
     any_ = pl.BlockSpec(memory_space=pl.ANY)

time: 69.2 us -> 66.6 us (0.962)
  Pallas kernels: 68.5 us -> 65.9 us
    pallas_call x1, Pallas kernels: 66.4 us -> 63.8 us  [step(): pl.pallas_call(kernel, out_shape=(jax.ShapeDtypeStruct((512, 512), BF), j...]
where the time goes in v4:
time: 66.6 us; the launch traced here: 66.5 us
  Pallas kernels  65.9 us (99%)
    pallas_call x1, Pallas kernels, step(): pl.pallas_call(kernel, out_shape=(jax.ShapeDtypeStruct((512, 512), BF), j...  63.8 us
    pallas_call x1, Pallas kernels, body(): pl.pallas_call(settle, out_shape=tuple((jax.ShapeDtypeStruct(*a) for a in...  2.06 us

profile of v4, /device:TPU:1, one launch (start us, length us, event | category | flops | bytes accessed | tf_op | source)
XLA Modules:
  0.0 66.5 jit_solution(1257889539428621544)
XLA Ops:
  0.6 63.8 %shard_map.67 = (bf16[512,512]{1,0:T(8,128)(2,1)}, f32[64,128]{1,0:T(8,128)}, f32[9,64,69]{2,1,0:T(8,128)}) custom-call(bf16[69,64,128]{2,1,0:T(8,128)(2,1)} %t_ref.1, bf16[9,64,69]{2,1,0:T(8,128)(2,1)} %bitcast.5, bf16[128,16384]{1,0:T(8,128)(2,1)} %w_ref.1, bf16[512,1024]{1,0:T(8,128)(2,1)} %bitcast.4), custom_call_target="tpu_custom_call" | custom-call | tf_op jit(solution)/shard_map/pallas_call | solution.py:538
  64.4 2.1 %shard_map.68 = (bf16[512,512]{1,0:T(8,128)(2,1)}, f32[64,128]{1,0:T(8,128)}, f32[9,64,69]{2,1,0:T(8,128)}) custom-call(bf16[512,512]{1,0:T(8,128)(2,1)} %get-tuple-element.9.emb, f32[64,128]{1,0:T(8,128)} %get-tuple-element.10.eg, f32[9,64,69]{2,1,0:T(8,128)} %get-tuple-element.11.cg), custom_call_target="tpu_custom_call" | custom-call | tf_op jit(solution)/shard_map/pallas_call | solution.py:575

commit v5 on v4

--- a/solution.py
+++ b/solution.py
@@ -244,7 +244,7 @@
 
     lax.fori_loop(0, 4, embed, 0, unroll=2)
     emb_copies = {}
-    for i in (4, 3, 5, 2, 6, 1, 7, 0):
+    for i in (1, 7, 4, 2, 6, 3, 5, 0):
         r = lax.rem(lo + i, 8)
         for g in range(2):
             emb_copies[i, g] = remote(

time: 66.6 us -> 66 us (level)
  Pallas kernels: 65.9 us -> 65.2 us
where the time goes in v5:
time: 66 us; the launch traced here: 65.9 us
  Pallas kernels  65.2 us (99%)
    pallas_call x1, Pallas kernels, step(): pl.pallas_call(kernel, out_shape=(jax.ShapeDtypeStruct((512, 512), BF), j...  63.2 us
    pallas_call x1, Pallas kernels, body(): pl.pallas_call(settle, out_shape=tuple((jax.ShapeDtypeStruct(*a) for a in...  2.06 us

profile of v5, /device:TPU:1, one launch (start us, length us, event | category | flops | bytes accessed | tf_op | source)
XLA Modules:
  0.0 65.9 jit_solution(4745532153379073085)
XLA Ops:
  0.6 63.2 %shard_map.67 = (bf16[512,512]{1,0:T(8,128)(2,1)}, f32[64,128]{1,0:T(8,128)}, f32[9,64,69]{2,1,0:T(8,128)}) custom-call(bf16[69,64,128]{2,1,0:T(8,128)(2,1)} %t_ref.1, bf16[9,64,69]{2,1,0:T(8,128)(2,1)} %bitcast.5, bf16[128,16384]{1,0:T(8,128)(2,1)} %w_ref.1, bf16[512,1024]{1,0:T(8,128)(2,1)} %bitcast.4), custom_call_target="tpu_custom_call" | custom-call | tf_op jit(solution)/shard_map/pallas_call | solution.py:538
  63.8 2.1 %shard_map.68 = (bf16[512,512]{1,0:T(8,128)(2,1)}, f32[64,128]{1,0:T(8,128)}, f32[9,64,69]{2,1,0:T(8,128)}) custom-call(bf16[512,512]{1,0:T(8,128)(2,1)} %get-tuple-element.9.emb, f32[64,128]{1,0:T(8,128)} %get-tuple-element.10.eg, f32[9,64,69]{2,1,0:T(8,128)} %get-tuple-element.11.cg), custom_call_target="tpu_custom_call" | custom-call | tf_op jit(solution)/shard_map/pallas_call | solution.py:575
